TPU v7x, 32 devices: a whole 2x2x4 slice. The times are simulated.
32 devices in a mesh: worker: 4 (over x, core), fsdp: 8 (over z, y).
Axes of the slice: x: 2, y: 2, z: 4, core: 2. Of those that a mesh axis runs over, the one named last changes fastest.
Arguments:
- inputs: bfloat16 [4, 2048, 8192], P('worker', 'fsdp'), may hold values from -6 to 6
- output_grads: bfloat16 [4, 2048, 1024], P('worker', 'fsdp'), may hold values from -0.3125 to 0.3125
- local_params: float32 [4, 8192, 1024], P('worker', 'fsdp'), may hold values from -6 to 6
- first_moment: float32 [4, 8192, 1024], P('worker', 'fsdp'), may hold values from -4 to 4
- second_moment: float32 [4, 8192, 1024], P('worker', 'fsdp'), may hold values from 0.01 to 0.1
- global_params: float32 [8192, 1024], P(('fsdp', 'worker')), may hold values from -6 to 6
- momentum: float32 [8192, 1024], P(('fsdp', 'worker')), may hold values from -6 to 6
Outputs:
- new_params: float32 [8192, 1024], P('fsdp')
- new_momentum: float32 [8192, 1024], P(('fsdp', 'worker'))
All inputs are finite; a program needn't handle non-finite values.
Results may differ from a plain program's by a relative error of at most 0.0015.
Values may be sent and summed in bfloat16 or wider, within the bound.
No kernel may reach another device: no remote copies, remote signals or barrier semaphores. Data moves between devices by JAX's collectives and lax.ppermute only.
A program may use at most 128 MiB of HBM per device.

v0:
```python
import jax
import jax.numpy as jnp
from jax import lax
from jax.sharding import PartitionSpec as P

beta_first = 0.8
beta_second = 0.9
inner_rate = 0.15
weight_decay = 0.1
adam_epsilon = 1e-08
outer_rate = 0.7
momentum_coef = 0.9
inner_count = 50


def shards(
    inputs, output_grads, local_params, first_moment, second_moment, global_params, momentum
):
    features = inputs[0]
    cotangents = output_grads[0]
    params = local_params[0]
    gradient = lax.psum_scatter(
        lax.dot_general(
            features, cotangents, (((0,), (0,)), ((), ())), preferred_element_type=jnp.float32
        ).astype(jnp.bfloat16),
        "fsdp",
        scatter_dimension=0,
        tiled=True,
    ).astype(jnp.float32)
    moment_one = beta_first * first_moment[0] + (1.0 - beta_first) * gradient
    moment_two = beta_second * second_moment[0] + (1.0 - beta_second) * gradient * gradient
    first_correction = 1.0 - beta_first**inner_count
    second_correction = 1.0 - beta_second**inner_count
    ratio = (
        moment_one / first_correction / (jnp.sqrt(moment_two / second_correction) + adam_epsilon)
    )
    stepped = params - inner_rate * (ratio + weight_decay * params)
    replicas = lax.axis_size("worker")
    anchor, moment_rows = (
        lax.all_gather(global_params, "worker", axis=0, tiled=True),
        lax.all_gather(momentum, "worker", axis=0, tiled=True),
    )
    pseudo_grad = anchor - stepped
    outer_grad = lax.psum(pseudo_grad, "worker") / replicas
    moment_full = momentum_coef * moment_rows + outer_grad
    fresh_rows = anchor - outer_rate * (outer_grad + momentum_coef * moment_full)
    share_rows = global_params.shape[0]
    worker_index = lax.axis_index("worker")
    own_moment = lax.dynamic_slice_in_dim(moment_full, worker_index * share_rows, share_rows, 0)
    return (fresh_rows, own_moment)


def solution(mesh):
    return jax.shard_map(
        shards,
        mesh=mesh,
        in_specs=(
            P("worker", "fsdp", None),
            P("worker", "fsdp", None),
            P("worker", "fsdp", None),
            P("worker", "fsdp", None),
            P("worker", "fsdp", None),
            P(("fsdp", "worker"), None),
            P(("fsdp", "worker"), None),
        ),
        out_specs=(P("fsdp", None), P(("fsdp", "worker"), None)),
        check_vma=False,
    )
```

profile of v0, /device:TPU:9, one launch (start us, length us, event | category | flops | bytes accessed | tf_op | source)
XLA Modules:
  0.0 411.4 jit_solution(12284738879164277884)
XLA Ops:
  8.0 0.0 copy-start
  8.0 0.0 all-gather.3.cloned.1.call-start
  8.1 0.7 all-gather.3.cloned.1.call-update
  8.7 0.0 reduce-scatter.2.cloned.1.call-start
  8.8 0.2 copy-done
  9.0 10.7 %convolution_convert_fusion = bf16[8192,1024]{1,0:T(8,128)(2,1)} fusion(bf16[1,256,8192]{2,1,0:T(8,128)(2,1)} %param.7, bf16[1,256,1024]{2,1,0:T(8,128)(2,1)S(1)} %copy-done), kind=kOutput, calls=%fused_computation | convolution fusion | flops 4303355904 | bytes 21495808 | tf_op jit(solution)/shard_map/dot_general | solution.py:23
  19.7 0.0 reduce-scatter.2.cloned.1.call-update
  19.8 0.0 all-gather.5.cloned.1.call-start
  19.8 0.7 all-gather.5.cloned.1.call-update
  20.5 0.0 all-reduce.2.cloned.1.call-start
  20.6 25.9 %all-gather.3.cloned.1.call-done = f32[1024,1024]{1,0:T(8,128)} async-done(((f32[256,1024]{1,0:T(8,128)}), f32[1024,1024]{1,0:T(8,128)}) %all-gather.3.cloned.1.call-update) | async-done | bytes 4194320 | tf_op jit(solution)/shard_map/all_gather | solution.py:40
  46.5 253.0 %reduce-scatter.2.cloned.1.call-done = bf16[1024,1024]{1,0:T(8,128)(2,1)} async-done(((bf16[8192,1024]{1,0:T(8,128)(2,1)}), bf16[1024,1024]{1,0:T(8,128)(2,1)}) %reduce-scatter.2.cloned.1.call-update) | async-done | bytes 2097168 | tf_op jit(solution)/shard_map/reduce_scatter | solution.py:22
  299.5 9.5 %fusion.6 = f32[1024,1024]{1,0:T(8,128)} fusion(f32[1024,1024]{1,0:T(8,128)} %all-gather.3.cloned.1.call-done, bf16[1024,1024]{1,0:T(8,128)(2,1)} %reduce-scatter.2.cloned.1.call-done, f32[1,1024,1024]{2,1,0:T(8,128)} %param.9, f32[1,1024,1024]{2,1,0:T(8,128)} %param.11, f32[1,1024,1024]{2,1,0:T(8,128)} %param.10), kind=kLoop, calls=%fused_computation.9 | loop fusion | flops 17825792 | bytes 23068672 | tf_op jit(solution)/shard_map/sub | solution.py:43
  309.0 0.0 all-reduce.2.cloned.1.call-update
  309.0 0.0 all-gather.5.cloned.1.call-done
  309.0 85.5 %all-reduce.2.cloned.1.call-done = f32[1024,1024]{1,0:T(8,128)} async-done(((f32[1024,1024]{1,0:T(8,128)}), f32[1024,1024]{1,0:T(8,128)}) %all-reduce.2.cloned.1.call-update) | async-done | bytes 4194320 | tf_op jit(solution)/shard_map/psum | solution.py:44
  394.5 8.7 %multiply_add_fusion = (f32[1024,1024]{1,0:T(8,128)S(1)}, f32[1024,1024]{1,0:T(8,128)}) fusion(f32[1024,1024]{1,0:T(8,128)} %all-gather.5.cloned.1.call-done, f32[1024,1024]{1,0:T(8,128)} %all-reduce.2.cloned.1.call-done, f32[1024,1024]{1,0:T(8,128)} %all-gather.3.cloned.1.call-done), kind=kLoop, calls=%fused_computation.17 | loop fusion | flops 7340032 | bytes 20971520 | tf_op jit(solution)/shard_map/add | solution.py:45
  403.3 1.0 constant_dynamic-slice_fusion
Async XLA Ops:
  8.0 1.0 copy-start
  8.0 38.5 %all-gather.3.cloned.1.call-start = ((), (), s32[]{:S(2)}) async-start(), calls=%async_computation.1 | async-start | bytes 5242880 | tf_op jit(solution)/shard_map/all_gather | solution.py:40
  8.7 290.8 %reduce-scatter.2.cloned.1.call-start = ((), (), s32[]{:S(2)}) async-start(), calls=%async_computation.2 | async-start | bytes 18874368 | tf_op jit(solution)/shard_map/reduce_scatter | solution.py:22
  19.8 289.3 %all-gather.5.cloned.1.call-start = ((), (), s32[]{:S(2)}) async-start(), calls=%async_computation.4 | async-start | bytes 5242880 | tf_op jit(solution)/shard_map/all_gather | solution.py:41
  20.5 374.0 %all-reduce.2.cloned.1.call-start = ((), (), s32[]{:S(2)}) async-start(), calls=%async_computation.3 | async-start | bytes 8388608 | tf_op jit(solution)/shard_map/psum | solution.py:44
Sparse Core Ops, SparseCore 0:
  10.4 36.0 all-gather.2
  48.0 34.5 all-gather.4
  309.1 85.3 all-reduce.1
Sparse Core Ops, SparseCore 1:
  19.9 279.6 reduce-scatter.1
where the time goes:
time: 413 us; the launch traced here: 411 us
  waiting for transfers between devices  366 us (89%)
  other arithmetic  18.2 us (4%)
  between operations  15.2 us (4%)
  matrix products  10.7 us (3%)
    reduce_scatter x1, waiting for transfers between devices, shards(): lax.psum_scatter(lax.dot_general(features, cotangents, (((0,), (0,)), (()...  253 us
    psum x1, waiting for transfers between devices, shards(): outer_grad = lax.psum(pseudo_grad, 'worker') / replicas  85.5 us
    all_gather x1, waiting for transfers between devices, shards(): lax.all_gather(global_params, 'worker', axis=0, tiled=True)  25.9 us
    dot_general x1, matrix products, shards(): lax.dot_general(features, cotangents, (((0,), (0,)), ((), ())), preferred...  10.7 us
    sub x1, other arithmetic, shards(): pseudo_grad = anchor - stepped  9.48 us
    add x1, other arithmetic, shards(): moment_full = momentum_coef * moment_rows + outer_grad  8.74 us
  transfers between devices with their start and end apart: 4, of which 3 were waited for; matrix products, arithmetic and copies ran while one was open for 5% of the time, Pallas kernels for 0%

commit v1 on v0

v1 whole, which is shorter than its diff:
```python
import functools
import math

import jax
import jax.numpy as jnp
from jax import lax
from jax.experimental import pallas as pl
from jax.experimental.pallas import tpu as pltpu
from jax.sharding import PartitionSpec as P

beta_first = 0.8
beta_second = 0.9
inner_rate = 0.15
weight_decay = 0.1
adam_epsilon = 1e-08
outer_rate = 0.7
momentum_coef = 0.9
inner_count = 50

TILE = 128
VMEM = 40 * 1024 * 1024


def chunks_of(rows):
    unit = 2 * TILE
    units = rows // unit
    sizes = [units - 1, 1] if units > 1 else [1]
    result, at = [], 0
    for size in sizes:
        result.append((at, size * unit))
        at += size * unit
    return result


def pairs(n, k, keep=lambda i: True):
    return [(i, i ^ k) for i in range(n) if keep(i)]


WINDOW = 5
COST = 4
PINNED = 2


class Mover:
    def __init__(self):
        self.done = []

    def __call__(self, v, axis, pairing):
        if len(self.done) >= WINDOW:
            v, _ = lax.optimization_barrier((v, self.done[-WINDOW]))
        arrived = lax.ppermute(v, axis, pairing)
        self.done.append(arrived)
        return arrived


def split_kernel(n, rows, pieces, info, x, *refs):
    outs, (buf, sem_in, sem_out) = refs[:-3], refs[-3:]
    reads, writes = [], []
    for k in range(n):
        start = pl.multiple_of((info[0] ^ k) * rows, TILE)
        reads.append(
            pltpu.make_async_copy(x.at[:, pl.ds(start, rows)], buf.at[k], sem_in.at[k])
        )
        reads[-1].start()
    for k in range(n):
        reads[k].wait()
        for j, (of, at, size) in enumerate(pieces):
            if of == k:
                copy = pltpu.make_async_copy(buf.at[k, :, pl.ds(at, size)], outs[j], sem_out.at[j])
                copy.start()
                writes.append(copy)
    for copy in writes:
        copy.wait()


def split_columns(info, x, n, rows, chunks):
    far = n // 2
    pieces = [(k, 0, rows) for k in range(far)]
    pieces += [(k, at, size) for at, size in chunks for k in range(far, n)]
    shapes = [jax.ShapeDtypeStruct((x.shape[0], size), x.dtype) for _, _, size in pieces]
    flat = pl.pallas_call(
        functools.partial(split_kernel, n, rows, pieces),
        in_specs=[pl.BlockSpec(memory_space=pltpu.SMEM), pl.BlockSpec(memory_space=pltpu.HBM)],
        out_specs=[pl.BlockSpec(memory_space=pltpu.HBM)] * len(shapes),
        scratch_shapes=[
            pltpu.VMEM((n, x.shape[0], rows), x.dtype),
            pltpu.SemaphoreType.DMA((n,)),
            pltpu.SemaphoreType.DMA((len(pieces),)),
        ],
        out_shape=shapes,
        compiler_params=pltpu.CompilerParams(vmem_limit_bytes=VMEM),
        name="split_columns",
    )(info, x)
    return flat[:far], [flat[far * (c + 1) : far * (c + 2)] for c in range(len(chunks))]


def exchange(move, block, whole, parts):
    n = lax.axis_size("fsdp")
    across = n // 4
    near, far = across, 2 * across
    gs = {0: block}
    xs = [{k: whole[k] for k in range(far)} for _ in parts]
    straight = [far, far + near]
    crossing = straight + [k for k in range(far, n) if k not in straight]

    def go(v, k):
        return move(v, "fsdp", pairs(n, k))

    def inside(*ks):
        for k in ks:
            arrived = go(whole[k], k)
            for x in xs:
                x[k] = arrived

    def cross(c, ks):
        for k in ks:
            xs[c][k] = go(parts[c][k - far], k)

    def spread(j):
        for k in range(1, across):
            gs[j + k] = go(gs[j], k)

    gs[far] = go(block, far)
    spread(0)
    inside(*range(1, across))
    gs[near] = go(block, near)
    cross(0, crossing[:1])
    gs[near + far] = go(gs[far], near)
    spread(far)
    cross(0, crossing[1:2])
    spread(near)
    inside(*range(near + 1, far))
    spread(near + far)
    cross(0, crossing[2:3])
    inside(near)
    cross(0, crossing[3:])
    for c in range(1, len(parts)):
        cross(c, crossing)
    return [gs[k] for k in range(n)], [[x[k] for k in range(n)] for x in xs], crossing


def step_kernel(n, half_tiles, at, share, scale, info, *refs):
    xs, gs = refs[:n], refs[n : 2 * n]
    params, first, second, anchor, momentum, send, keep = refs[2 * n :]
    gradient = None
    for x, g in zip(xs, gs):
        term = lax.dot_general(
            x[...], g[...], (((0,), (0,)), ((), ())), preferred_element_type=jnp.float32
        )
        gradient = term if gradient is None else gradient + term
    moment_one = beta_first * first[...] + (1.0 - beta_first) * gradient
    moment_two = beta_second * second[...] + (1.0 - beta_second) * gradient * gradient
    first_correction = 1.0 - beta_first**inner_count
    second_correction = 1.0 - beta_second**inner_count
    ratio = (
        moment_one
        * (1.0 / first_correction)
        / (jnp.sqrt(moment_two * (1.0 / second_correction)) + adam_epsilon)
    )
    stepped = params[...] - inner_rate * (ratio + weight_decay * params[...])
    i = pl.program_id(0)
    piece = min(share, TILE)
    offset = info[2] * share - (at + step_tile(i, info, half_tiles) * TILE)
    inside = (offset > -share) & (offset < TILE)

    def store(out):
        out[...] = stepped

        @pl.when(inside)
        def _():
            rows = pl.ds(pl.multiple_of(jnp.maximum(offset, 0), piece), piece)
            out[rows] += owner_term(anchor[...], momentum[...], scale)

    pl.when(i < half_tiles)(lambda: store(send))
    pl.when(i >= half_tiles)(lambda: store(keep))


def owner_term(anchor, momentum, scale):
    step = outer_rate * (1.0 + momentum_coef)
    return (scale * (1.0 - step) / step) * anchor - (
        scale * outer_rate * momentum_coef**2 / step
    ) * momentum


def step_tile(i, info, half_tiles):
    core = info[1]
    return jnp.where(i < half_tiles, (1 - core) * half_tiles + i, core * half_tiles + i - half_tiles)


def inner_step(info, xs, gs, params, first, second, anchor, momentum, scale, at, size):
    n = len(gs)
    tokens, width = gs[0].shape
    share = anchor.shape[0]
    half_tiles = size // TILE // 2
    piece = min(share, TILE)

    def tile(i, info):
        return step_tile(i, info, half_tiles)

    def owned(i, info):
        ahead = at + tile(i, info) * TILE - info[2] * share
        return (jnp.clip(ahead // piece, 0, share // piece - 1), 0)

    columns = [
        pl.BlockSpec(
            (tokens, TILE),
            lambda i, info, skip=0 if x.shape[1] == size else at // TILE: (0, skip + tile(i, info)),
        )
        for x in xs
    ]
    whole = pl.BlockSpec((tokens, width), lambda i, info: (0, 0))
    state = pl.BlockSpec((None, TILE, width), lambda i, info: (0, at // TILE + tile(i, info), 0))
    shape = jax.ShapeDtypeStruct((size // 2, width), jnp.float32)
    return pl.pallas_call(
        functools.partial(step_kernel, n, half_tiles, at, share, scale),
        grid_spec=pltpu.PrefetchScalarGridSpec(
            num_scalar_prefetch=1,
            grid=(2 * half_tiles,),
            in_specs=columns
            + [whole] * n
            + [state] * 3
            + [pl.BlockSpec((piece, width), owned)] * 2,
            out_specs=[
                pl.BlockSpec((TILE, width), lambda i, info: (jnp.minimum(i, half_tiles - 1), 0)),
                pl.BlockSpec((TILE, width), lambda i, info: (jnp.maximum(i - half_tiles, 0), 0)),
            ],
        ),
        out_shape=[shape, shape],
        compiler_params=pltpu.CompilerParams(vmem_limit_bytes=VMEM),
        cost_estimate=pl.CostEstimate(
            flops=COST * 2 * n * tokens * size * width,
            bytes_accessed=COST * 4 * size * width * 5,
            transcendentals=COST * size * width,
        ),
        name="inner_step",
    )(info, *xs, *gs, params, first, second, anchor, momentum)


def outer_kernel(at, half, share, info, mine, other, anchor, momentum, *refs):
    whole, fresh, buf, sem = refs[-4:]
    core, worker = info[1], info[2]
    copies = []
    for j, (source, side) in enumerate(((mine, core), (other, 1 - core))):
        rows = pl.ds(pl.multiple_of(at + side * half, TILE), half)
        copies.append(pltpu.make_async_copy(source, whole.at[rows], sem.at[j]))
        copies[-1].start()
    first = worker * share - at
    step = outer_rate * (1.0 + momentum_coef)

    @pl.when((first >= 0) & (first < 2 * half))
    def _():
        piece = math.gcd(share, half)
        for p in range(share // piece):
            row = first + p * piece
            side = row // half
            rows = pl.ds(pl.multiple_of(row - side * half, piece), piece)
            part = pl.ds(p * piece, piece)

            def momentum_of(source):
                buf[part] = (
                    (momentum_coef - outer_rate * momentum_coef**2 / step) * momentum[part]
                    + (1.0 + (1.0 - step) / step) * anchor[part]
                    - (1.0 / step) * source[rows]
                )

            pl.when(side == core)(lambda: momentum_of(mine))
            pl.when(side != core)(lambda: momentum_of(other))
        copy = pltpu.make_async_copy(buf, fresh, sem.at[2])
        copy.start()
        copy.wait()

    for copy in copies:
        copy.wait()


def outer_step(info, mine, other, anchor, momentum, state, rows, at):
    half, width = mine.shape
    share = anchor.shape[0]
    shapes = [
        jax.ShapeDtypeStruct((rows, width), jnp.float32),
        jax.ShapeDtypeStruct((share, width), jnp.float32),
    ]
    return pl.pallas_call(
        functools.partial(outer_kernel, at, half, share),
        in_specs=[pl.BlockSpec(memory_space=pltpu.SMEM)]
        + [pl.BlockSpec(memory_space=pltpu.VMEM)] * 4
        + [pl.BlockSpec(memory_space=pl.ANY)] * len(state),
        out_specs=[pl.BlockSpec(memory_space=pl.ANY)] * 2,
        out_shape=shapes,
        scratch_shapes=[
            pltpu.VMEM((share, width), jnp.float32),
            pltpu.SemaphoreType.DMA((3,)),
        ],
        input_output_aliases={5: 0, 6: 1} if state else {},
        compiler_params=pltpu.CompilerParams(vmem_limit_bytes=VMEM),
        name="outer_step",
    )(info, mine, other, anchor, momentum, *state)


def shards(
    inputs, output_grads, local_params, first_moment, second_moment, global_params, momentum
):
    n, replicas = lax.axis_size("fsdp"), lax.axis_size("worker")
    me, worker = lax.axis_index("fsdp"), lax.axis_index("worker")
    info = jnp.stack([me, worker % 2, worker]).astype(jnp.int32)
    features = inputs[0]
    rows = local_params.shape[1]
    chunks = chunks_of(rows)
    step = outer_rate * (1.0 + momentum_coef)

    own, parts = split_columns(info, features, n, rows, chunks)
    block, own, parts = lax.optimization_barrier((output_grads[0], own, parts))
    gs, columns, ks = exchange(Mover(), block, own, parts)
    state = []
    for c, (at, size) in enumerate(chunks):
        xs = columns[c]
        send, keep = inner_step(
            info,
            xs,
            gs,
            local_params,
            first_moment,
            second_moment,
            global_params,
            momentum,
            float(replicas),
            at,
            size,
        )
        if c + 1 < len(chunks):
            pinned = [columns[c + 1][k] for k in ks[:PINNED]]
            send, keep, _ = lax.optimization_barrier((send, keep, pinned))
        total = keep + lax.ppermute(send, "worker", pairs(replicas, 1))
        k = 2
        while k < replicas:
            half = total.astype(jnp.float16)
            got = lax.ppermute(half, "worker", pairs(replicas, k))
            if k * 2 >= replicas and c + 1 == len(chunks):
                got, state = lax.optimization_barrier((got, state))
            total = half.astype(jnp.float32) + got.astype(jnp.float32)
            k *= 2
        mine = total * (step / replicas)
        other = lax.ppermute(mine, "worker", pairs(replicas, 1))
        state = outer_step(info, mine, other, global_params, momentum, state, rows, at)
    return tuple(state)


def solution(mesh):
    return jax.shard_map(
        shards,
        mesh=mesh,
        in_specs=(
            P("worker", "fsdp", None),
            P("worker", "fsdp", None),
            P("worker", "fsdp", None),
            P("worker", "fsdp", None),
            P("worker", "fsdp", None),
            P(("fsdp", "worker"), None),
            P(("fsdp", "worker"), None),
        ),
        out_specs=(P("fsdp", None), P(("fsdp", "worker"), None)),
        check_vma=False,
    )
```

time: 413 us -> 168 us (0.41)
  waiting for transfers between devices: 366 us -> 111 us
  starting transfers between devices: 0.16 us -> 30.9 us
  Pallas kernels: 0 us -> 20.7 us
  other arithmetic: 18.2 us -> 0.96 us
  between operations: 15.2 us -> 0.74 us
  matrix products: 10.7 us -> 0 us
    reduce_scatter x1 -> x0, waiting for transfers between devices: 253 us -> none  [shards(): lax.psum_scatter(lax.dot_general(features, cotangents, (((0,), (0,)), (()...]
    ppermute x0 -> x24, waiting for transfers between devices: none -> 111 us  [the longest x18 85.8 us: __call__(): arrived = lax.ppermute(v, axis, pairing)]
    psum x1 -> x0, waiting for transfers between devices: 85.5 us -> none  [shards(): outer_grad = lax.psum(pseudo_grad, 'worker') / replicas]
    ppermute x0 -> x24, starting transfers between devices: none -> 30.9 us  [the longest x18 21 us: __call__(): arrived = lax.ppermute(v, axis, pairing)]
    all_gather x2 -> x0, waiting for transfers between devices: 25.9 us -> none  [the longest x1 25.9 us: shards(): lax.all_gather(global_params, 'worker', axis=0, tiled=True)]
    pallas_call x0 -> x5, Pallas kernels: none -> 20.7 us  [the longest x2 15.1 us: inner_step(): pl.pallas_call(functools.partial(step_kernel, n, half_tiles, at, share, s...]
    dot_general x1 -> x0, matrix products: 10.7 us -> none  [shards(): lax.dot_general(features, cotangents, (((0,), (0,)), ((), ())), preferred...]
    sub x1 -> x0, other arithmetic: 9.48 us -> none  [shards(): pseudo_grad = anchor - stepped]
  transfers between devices with their start and end apart: 4 -> 24, of which waited for: 3 -> 12; matrix products, arithmetic and copies ran while one was open for 5% -> 0% of each run, Pallas kernels for 0% -> 11%
where the time goes in v1:
time: 168 us; the launch traced here: 167 us
  waiting for transfers between devices  111 us (66%)
  starting transfers between devices  30.9 us (18%)
  Pallas kernels  20.7 us (12%)
  local copies, waits for them, and re-layouts  2.2 us (1%)
    ppermute x18, waiting for transfers between devices, __call__(): arrived = lax.ppermute(v, axis, pairing)  85.8 us
    ppermute x18, starting transfers between devices, __call__(): arrived = lax.ppermute(v, axis, pairing)  21 us
    ppermute x2, waiting for transfers between devices, shards(): got = lax.ppermute(half, 'worker', pairs(replicas, k))  19.1 us
    pallas_call x2, Pallas kernels, inner_step(): pl.pallas_call(functools.partial(step_kernel, n, half_tiles, at, share, s...  15.1 us
    ppermute x2, waiting for transfers between devices, shards(): total = keep + lax.ppermute(send, 'worker', pairs(replicas, 1))  4.91 us
    ppermute x2, starting transfers between devices, shards(): total = keep + lax.ppermute(send, 'worker', pairs(replicas, 1))  4.75 us
    pallas_call x2, Pallas kernels, outer_step(): pl.pallas_call(functools.partial(outer_kernel, at, half, share), in_specs...  4.11 us
  transfers between devices with their start and end apart: 24, of which 12 were waited for; matrix products, arithmetic and copies ran while one was open for 0% of the time, Pallas kernels for 11%

profile of v1, /device:TPU:9, one launch (start us, length us, event | category | flops | bytes accessed | tf_op | source)
XLA Modules:
  0.0 166.9 jit_solution(2549823667533207580)
XLA Ops:
  0.6 0.1 pad_add_fusion.info
  0.7 2.2 %copy-done.2 = bf16[1,256,8192]{2,1,0:T(8,128)(2,1)S(1)} copy-done((bf16[1,256,8192]{2,1,0:T(8,128)(2,1)S(1)}, bf16[1,256,8192]{2,1,0:T(8,128)(2,1)}, u32[]{:S(2)}) %copy-start.2) | copy-done | bytes 4194328
  2.9 1.5 split_columns.1
  4.4 2.4 %collective-permute-start.6 = (bf16[256,1024]{1,0:T(8,128)(2,1)S(1)}, bf16[256,1024]{1,0:T(8,128)(2,1)S(1)}, u32[]{:S(2)}, u32[]{:S(2)}) collective-permute-start(bf16[256,1024]{1,0:T(8,128)(2,1)S(1)} %bitcast.6), channel_id=1, source_target_pairs={{0,4},{1,5},{2,6},{3,7},{4,0},{5,1},{6,2},{7,3},{8,12},{9,13},{10,... | collective-permute-start | bytes 1572872 | tf_op jit(solution)/shard_map/ppermute | solution.py:51
  6.8 1.2 collective-permute-start
  8.0 0.2 collective-permute-start.7
  8.3 0.2 collective-permute-start.15
  8.4 21.2 %collective-permute-done.6.refs_12_ = bf16[256,1024]{1,0:T(8,128)(2,1)S(1)} collective-permute-done((bf16[256,1024]{1,0:T(8,128)(2,1)S(1)}, bf16[256,1024]{1,0:T(8,128)(2,1)S(1)}, u32[]{:S(2)}, u32[]{:S(2)}) %collective-permute-start.6) | collective-permute-done | bytes 524320 | tf_op jit(solution)/shard_map/ppermute | solution.py:51
  29.6 0.3 collective-permute-start.11
  29.9 2.8 %collective-permute-start.3 = (bf16[256,768]{1,0:T(8,128)(2,1)S(1)}, bf16[256,768]{1,0:T(8,128)(2,1)S(1)}, u32[]{:S(2)}, u32[]{:S(2)}) collective-permute-start(bf16[256,768]{1,0:T(8,128)(2,1)S(1)} %get-tuple-element.70), channel_id=1, source_target_pairs={{0,4},{1,5},{2,6},{3,7},{4,0},{5,1},{6,2},{7,3},{8,12},{9,13},{10,... | collective-permute-start | bytes 1179656 | tf_op jit(solution)/shard_map/ppermute | solution.py:51
  32.7 0.0 collective-permute-done.refs_1_
  32.7 0.0 collective-permute-done.7.refs_9_
  32.7 1.2 collective-permute-start.8
  34.0 0.0 collective-permute-done.15.refs_10_
  34.0 0.2 collective-permute-start.16
  34.2 0.3 collective-permute-start.1
  34.5 18.4 %collective-permute-done.3.refs_4_ = bf16[256,768]{1,0:T(8,128)(2,1)S(1)} collective-permute-done((bf16[256,768]{1,0:T(8,128)(2,1)S(1)}, bf16[256,768]{1,0:T(8,128)(2,1)S(1)}, u32[]{:S(2)}, u32[]{:S(2)}) %collective-permute-start.3) | collective-permute-done | bytes 393248 | tf_op jit(solution)/shard_map/ppermute | solution.py:51
  53.0 1.2 collective-permute-start.12
  54.2 12.8 %collective-permute-done.1.refs_6_ = bf16[256,768]{1,0:T(8,128)(2,1)S(1)} collective-permute-done((bf16[256,768]{1,0:T(8,128)(2,1)S(1)}, bf16[256,768]{1,0:T(8,128)(2,1)S(1)}, u32[]{:S(2)}, u32[]{:S(2)}) %collective-permute-start.1) | collective-permute-done | bytes 393248 | tf_op jit(solution)/shard_map/ppermute | solution.py:51
  67.0 0.0 collective-permute-done.8.refs_13_
  67.0 3.4 %collective-permute-start.9 = (bf16[256,768]{1,0:T(8,128)(2,1)S(1)}, bf16[256,768]{1,0:T(8,128)(2,1)S(1)}, u32[]{:S(2)}, u32[]{:S(2)}) collective-permute-start(bf16[256,768]{1,0:T(8,128)(2,1)S(1)} %get-tuple-element.78), channel_id=1, source_target_pairs={{0,5},{1,4},{2,7},{3,6},{4,1},{5,0},{6,3},{7,2},{8,13},{9,12},{10,... | collective-permute-start | bytes 1179656 | tf_op jit(solution)/shard_map/ppermute | solution.py:51
  70.4 0.2 collective-permute-start.19
  70.6 9.0 %collective-permute-done.4.refs_3_ = bf16[256,1024]{1,0:T(8,128)(2,1)S(1)} collective-permute-done((bf16[256,1024]{1,0:T(8,128)(2,1)S(1)}, bf16[256,1024]{1,0:T(8,128)(2,1)S(1)}, u32[]{:S(2)}, u32[]{:S(2)}) %collective-permute-start.4) | collective-permute-done | bytes 524320 | tf_op jit(solution)/shard_map/ppermute | solution.py:51
  79.5 0.4 collective-permute-done.12.refs_15_
  79.9 5.2 %collective-permute-start.13 = (bf16[256,256]{1,0:T(8,128)(2,1)S(1)}, bf16[256,256]{1,0:T(8,128)(2,1)S(1)}, u32[]{:S(2)}, u32[]{:S(2)}) collective-permute-start(bf16[256,256]{1,0:T(8,128)(2,1)S(1)} %get-tuple-element.83), channel_id=1, source_target_pairs={{0,6},{1,7},{2,4},{3,5},{4,2},{5,3},{6,0},{7,1},{8,14},{9,15},{10,... | collective-permute-start | bytes 393224 | tf_op jit(solution)/shard_map/ppermute | solution.py:51
  85.1 7.4 %collective-permute-done.9.refs_5_ = bf16[256,768]{1,0:T(8,128)(2,1)S(1)} collective-permute-done((bf16[256,768]{1,0:T(8,128)(2,1)S(1)}, bf16[256,768]{1,0:T(8,128)(2,1)S(1)}, u32[]{:S(2)}, u32[]{:S(2)}) %collective-permute-start.9) | collective-permute-done | bytes 393248 | tf_op jit(solution)/shard_map/ppermute | solution.py:51
  92.5 16.6 %collective-permute-done.19.refs_7_ = bf16[256,768]{1,0:T(8,128)(2,1)S(1)} collective-permute-done((bf16[256,768]{1,0:T(8,128)(2,1)S(1)}, bf16[256,768]{1,0:T(8,128)(2,1)S(1)}, u32[]{:S(2)}, u32[]{:S(2)}) %collective-permute-start.19) | collective-permute-done | bytes 393248 | tf_op jit(solution)/shard_map/ppermute | solution.py:51
  109.1 0.0 collective-permute-done.2.refs_2_
  109.1 10.7 %inner_step.3 = (f32[384,1024]{1,0:T(8,128)S(1)}, f32[384,1024]{1,0:T(8,128)S(1)}) custom-call(s32[3]{0:T(128)S(1)} %pad_add_fusion.info, bf16[256,1024]{1,0:T(8,128)(2,1)S(1)} %get-tuple-element.63.refs_0_, bf16[256,1024]{1,0:T(8,128)(2,1)S(1)} %collective-permute-done.refs_1_, bf16[256,1024]{1,0:T(8,128)(2,1)S(1)} %collective-permute-done.2.refs_2_, ...), custom_call_target="tpu_custom_call" | custom-call | flops 12884901888 | bytes 62914560 | tf_op jit(solution)/shard_map/inner_step/pallas_call | solution.py:214
  119.8 4.7 %collective-permute-start.20 = (f32[384,1024]{1,0:T(8,128)S(1)}, f32[384,1024]{1,0:T(8,128)S(1)}, u32[]{:S(2)}, u32[]{:S(2)}) collective-permute-start(f32[384,1024]{1,0:T(8,128)S(1)} %get-tuple-element.94), channel_id=1, source_target_pairs={{0,8},{8,0},{16,24},{24,16},{1,9},{9,1},{17,25},{25,17},{2,10},{10... | collective-permute-start | bytes 4718600 | tf_op jit(solution)/shard_map/ppermute | solution.py:333
  124.4 3.0 %collective-permute-done.20 = f32[384,1024]{1,0:T(8,128)S(1)} collective-permute-done((f32[384,1024]{1,0:T(8,128)S(1)}, f32[384,1024]{1,0:T(8,128)S(1)}, u32[]{:S(2)}, u32[]{:S(2)}) %collective-permute-start.20) | collective-permute-done | bytes 1572896 | tf_op jit(solution)/shard_map/ppermute | solution.py:333
  127.5 0.3 add_convert_fusion
  127.8 1.3 collective-permute-start.21
  129.2 2.1 %collective-permute-start.14 = (bf16[256,256]{1,0:T(8,128)(2,1)S(1)}, bf16[256,256]{1,0:T(8,128)(2,1)S(1)}, u32[]{:S(2)}, u32[]{:S(2)}) collective-permute-start(bf16[256,256]{1,0:T(8,128)(2,1)S(1)} %get-tuple-element.85), channel_id=1, source_target_pairs={{0,7},{1,6},{2,5},{3,4},{4,3},{5,2},{6,1},{7,0},{8,15},{9,14},{10,... | collective-permute-start | bytes 393224 | tf_op jit(solution)/shard_map/ppermute | solution.py:51
  131.3 15.3 %collective-permute-done.21 = f16[384,1024]{1,0:T(8,128)(2,1)S(1)} collective-permute-done((f16[384,1024]{1,0:T(8,128)(2,1)S(1)}, f16[384,1024]{1,0:T(8,128)(2,1)S(1)}, u32[]{:S(2)}, u32[]{:S(2)}) %collective-permute-start.21) | collective-permute-done | bytes 786464 | tf_op jit(solution)/shard_map/ppermute | solution.py:337
  146.7 0.4 add_multiply_fusion.mine
  147.0 1.3 collective-permute-start.22
  148.3 4.5 %inner_step.2 = (f32[128,1024]{1,0:T(8,128)S(1)}, f32[128,1024]{1,0:T(8,128)S(1)}) custom-call(s32[3]{0:T(128)S(1)} %pad_add_fusion.info, bf16[256,1024]{1,0:T(8,128)(2,1)S(1)} %get-tuple-element.63.refs_0_, bf16[256,1024]{1,0:T(8,128)(2,1)S(1)} %collective-permute-done.refs_1_, bf16[256,1024]{1,0:T(8,128)(2,1)S(1)} %collective-permute-done.2.refs_2_, ...), custom_call_target="tpu_custom_call" | custom-call | flops 4294967296 | bytes 20971520 | tf_op jit(solution)/shard_map/inner_step/pallas_call | solution.py:214
  152.8 0.1 collective-permute-start.17
  152.9 1.9 %collective-permute-done.17 = f32[128,1024]{1,0:T(8,128)S(1)} collective-permute-done((f32[128,1024]{1,0:T(8,128)S(1)}, f32[128,1024]{1,0:T(8,128)S(1)}, u32[]{:S(2)}, u32[]{:S(2)}) %collective-permute-start.17) | collective-permute-done | bytes 524320 | tf_op jit(solution)/shard_map/ppermute | solution.py:333
  154.8 0.1 add_convert_fusion.1
  154.8 1.5 collective-permute-start.18
  156.4 2.6 %outer_step.2 = (f32[1024,1024]{1,0:T(8,128)}, f32[256,1024]{1,0:T(8,128)}) custom-call(s32[3]{0:T(128)S(1)} %pad_add_fusion.info, f32[384,1024]{1,0:T(8,128)S(1)} %add_multiply_fusion.mine, f32[384,1024]{1,0:T(8,128)S(1)} %collective-permute-done.22.other, f32[256,1024]{1,0:T(8,128)S(1)} %copy-done, f32[256,1024]{1,0:T(8,128)S(1)} %copy-done.1), custom_call_target="tpu_custom_call" | custom-call | tf_op jit(solution)/shard_map/outer_step/pallas_call | solution.py:283
  159.0 3.7 %collective-permute-done.18 = f16[128,1024]{1,0:T(8,128)(2,1)S(1)} collective-permute-done((f16[128,1024]{1,0:T(8,128)(2,1)S(1)}, f16[128,1024]{1,0:T(8,128)(2,1)S(1)}, u32[]{:S(2)}, u32[]{:S(2)}) %collective-permute-start.18) | collective-permute-done | bytes 262176 | tf_op jit(solution)/shard_map/ppermute | solution.py:337
  162.7 0.1 add_multiply_fusion.1.mine
  162.8 1.0 collective-permute-start.23
  163.8 1.5 collective-permute-done.23.other
  165.3 1.5 outer_step.3
  (20 shorter events, 0.0 us)
Async XLA Ops:
  0.7 2.2 %copy-start.2 = (bf16[1,256,8192]{2,1,0:T(8,128)(2,1)S(1)}, bf16[1,256,8192]{2,1,0:T(8,128)(2,1)}, u32[]{:S(2)}) copy-start(bf16[1,256,8192]{2,1,0:T(8,128)(2,1)} %param.7) | copy-start | bytes 12582916
  2.9 1.5 copy-start.4
  2.9 106.2 %copy-start = (f32[256,1024]{1,0:T(8,128)S(1)}, f32[256,1024]{1,0:T(8,128)}, u32[]{:S(2)}) copy-start(f32[256,1024]{1,0:T(8,128)} %anchor.3) | copy-start | bytes 3145732
  2.9 106.2 %copy-start.1 = (f32[256,1024]{1,0:T(8,128)S(1)}, f32[256,1024]{1,0:T(8,128)}, u32[]{:S(2)}) copy-start(f32[256,1024]{1,0:T(8,128)} %momentum.3) | copy-start | bytes 3145732
  4.4 25.2 %collective-permute-start.6 = (bf16[256,1024]{1,0:T(8,128)(2,1)S(1)}, bf16[256,1024]{1,0:T(8,128)(2,1)S(1)}, u32[]{:S(2)}, u32[]{:S(2)}) collective-permute-start(bf16[256,1024]{1,0:T(8,128)(2,1)S(1)} %bitcast.6), channel_id=1, source_target_pairs={{0,4},{1,5},{2,6},{3,7},{4,0},{5,1},{6,2},{7,3},{8,12},{9,13},{10,... | collective-permute-start | bytes 1572872 | tf_op jit(solution)/shard_map/ppermute | solution.py:51
  6.8 25.9 %collective-permute-start = (bf16[256,1024]{1,0:T(8,128)(2,1)S(1)}, bf16[256,1024]{1,0:T(8,128)(2,1)S(1)}, u32[]{:S(2)}, u32[]{:S(2)}) collective-permute-start(bf16[256,1024]{1,0:T(8,128)(2,1)S(1)} %get-tuple-element.64), channel_id=1, source_target_pairs={{0,1},{1,0},{2,3},{3,2},{4,5},{5,4},{6,7},{7,6},{8,9},{9,8},{10,11... | collective-permute-start | bytes 1572872 | tf_op jit(solution)/shard_map/ppermute | solution.py:51
  8.0 24.7 %collective-permute-start.7 = (bf16[256,1024]{1,0:T(8,128)(2,1)S(1)}, bf16[256,1024]{1,0:T(8,128)(2,1)S(1)}, u32[]{:S(2)}, u32[]{:S(2)}) collective-permute-start(bf16[256,1024]{1,0:T(8,128)(2,1)S(1)} %bitcast.7), channel_id=1, source_target_pairs={{0,1},{1,0},{2,3},{3,2},{4,5},{5,4},{6,7},{7,6},{8,9},{9,8},{10,11... | collective-permute-start | bytes 1572872 | tf_op jit(solution)/shard_map/ppermute | solution.py:51
  8.3 25.7 %collective-permute-start.15 = (bf16[256,1024]{1,0:T(8,128)(2,1)S(1)}, bf16[256,1024]{1,0:T(8,128)(2,1)S(1)}, u32[]{:S(2)}, u32[]{:S(2)}) collective-permute-start(bf16[256,1024]{1,0:T(8,128)(2,1)S(1)} %bitcast.8), channel_id=1, source_target_pairs={{0,2},{1,3},{2,0},{3,1},{4,6},{5,7},{6,4},{7,5},{8,10},{9,11},{10,... | collective-permute-start | bytes 1572872 | tf_op jit(solution)/shard_map/ppermute | solution.py:51
  29.6 23.4 %collective-permute-start.11 = (bf16[256,1024]{1,0:T(8,128)(2,1)S(1)}, bf16[256,1024]{1,0:T(8,128)(2,1)S(1)}, u32[]{:S(2)}, u32[]{:S(2)}) collective-permute-start(bf16[256,1024]{1,0:T(8,128)(2,1)S(1)} %collective-permute-done.6.refs_12_), channel_id=1, source_target_pairs={{0,2},{1,3},{2,0},{3,1},{4,6},{5,7},{6,4},{7,5},{8,10},{9,11},{10,... | collective-permute-start | bytes 1572872 | tf_op jit(solution)/shard_map/ppermute | solution.py:51
  29.9 23.1 %collective-permute-start.3 = (bf16[256,768]{1,0:T(8,128)(2,1)S(1)}, bf16[256,768]{1,0:T(8,128)(2,1)S(1)}, u32[]{:S(2)}, u32[]{:S(2)}) collective-permute-start(bf16[256,768]{1,0:T(8,128)(2,1)S(1)} %get-tuple-element.70), channel_id=1, source_target_pairs={{0,4},{1,5},{2,6},{3,7},{4,0},{5,1},{6,2},{7,3},{8,12},{9,13},{10,... | collective-permute-start | bytes 1179656 | tf_op jit(solution)/shard_map/ppermute | solution.py:51
  32.7 34.3 %collective-permute-start.8 = (bf16[256,1024]{1,0:T(8,128)(2,1)S(1)}, bf16[256,1024]{1,0:T(8,128)(2,1)S(1)}, u32[]{:S(2)}, u32[]{:S(2)}) collective-permute-start(bf16[256,1024]{1,0:T(8,128)(2,1)S(1)} %collective-permute-done.6.refs_12_), channel_id=1, source_target_pairs={{0,1},{1,0},{2,3},{3,2},{4,5},{5,4},{6,7},{7,6},{8,9},{9,8},{10,11... | collective-permute-start | bytes 1572872 | tf_op jit(solution)/shard_map/ppermute | solution.py:51
  34.0 36.4 %collective-permute-start.16 = (bf16[256,1024]{1,0:T(8,128)(2,1)S(1)}, bf16[256,1024]{1,0:T(8,128)(2,1)S(1)}, u32[]{:S(2)}, u32[]{:S(2)}) collective-permute-start(bf16[256,1024]{1,0:T(8,128)(2,1)S(1)} %collective-permute-done.15.refs_10_), channel_id=1, source_target_pairs={{0,1},{1,0},{2,3},{3,2},{4,5},{5,4},{6,7},{7,6},{8,9},{9,8},{10,11... | collective-permute-start | bytes 1572872 | tf_op jit(solution)/shard_map/ppermute | solution.py:51
  34.2 32.8 %collective-permute-start.1 = (bf16[256,768]{1,0:T(8,128)(2,1)S(1)}, bf16[256,768]{1,0:T(8,128)(2,1)S(1)}, u32[]{:S(2)}, u32[]{:S(2)}) collective-permute-start(bf16[256,768]{1,0:T(8,128)(2,1)S(1)} %get-tuple-element.67), channel_id=1, source_target_pairs={{0,6},{1,7},{2,4},{3,5},{4,2},{5,3},{6,0},{7,1},{8,14},{9,15},{10,... | collective-permute-start | bytes 1179656 | tf_op jit(solution)/shard_map/ppermute | solution.py:51
  53.0 26.6 %collective-permute-start.4 = (bf16[256,1024]{1,0:T(8,128)(2,1)S(1)}, bf16[256,1024]{1,0:T(8,128)(2,1)S(1)}, u32[]{:S(2)}, u32[]{:S(2)}) collective-permute-start(bf16[256,1024]{1,0:T(8,128)(2,1)S(1)} %get-tuple-element.71), channel_id=1, source_target_pairs={{0,3},{1,2},{2,1},{3,0},{4,7},{5,6},{6,5},{7,4},{8,11},{9,10},{10,... | collective-permute-start | bytes 1572872 | tf_op jit(solution)/shard_map/ppermute | solution.py:51
  53.0 26.9 %collective-permute-start.12 = (bf16[256,1024]{1,0:T(8,128)(2,1)S(1)}, bf16[256,1024]{1,0:T(8,128)(2,1)S(1)}, u32[]{:S(2)}, u32[]{:S(2)}) collective-permute-start(bf16[256,1024]{1,0:T(8,128)(2,1)S(1)} %collective-permute-done.11.refs_14_), channel_id=1, source_target_pairs={{0,1},{1,0},{2,3},{3,2},{4,5},{5,4},{6,7},{7,6},{8,9},{9,8},{10,11... | collective-permute-start | bytes 1572872 | tf_op jit(solution)/shard_map/ppermute | solution.py:51
  67.0 42.1 %collective-permute-start.2 = (bf16[256,1024]{1,0:T(8,128)(2,1)S(1)}, bf16[256,1024]{1,0:T(8,128)(2,1)S(1)}, u32[]{:S(2)}, u32[]{:S(2)}) collective-permute-start(bf16[256,1024]{1,0:T(8,128)(2,1)S(1)} %get-tuple-element.68), channel_id=1, source_target_pairs={{0,2},{1,3},{2,0},{3,1},{4,6},{5,7},{6,4},{7,5},{8,10},{9,11},{10,... | collective-permute-start | bytes 1572872 | tf_op jit(solution)/shard_map/ppermute | solution.py:51
  67.0 25.5 %collective-permute-start.9 = (bf16[256,768]{1,0:T(8,128)(2,1)S(1)}, bf16[256,768]{1,0:T(8,128)(2,1)S(1)}, u32[]{:S(2)}, u32[]{:S(2)}) collective-permute-start(bf16[256,768]{1,0:T(8,128)(2,1)S(1)} %get-tuple-element.78), channel_id=1, source_target_pairs={{0,5},{1,4},{2,7},{3,6},{4,1},{5,0},{6,3},{7,2},{8,13},{9,12},{10,... | collective-permute-start | bytes 1179656 | tf_op jit(solution)/shard_map/ppermute | solution.py:51
  70.4 38.7 %collective-permute-start.19 = (bf16[256,768]{1,0:T(8,128)(2,1)S(1)}, bf16[256,768]{1,0:T(8,128)(2,1)S(1)}, u32[]{:S(2)}, u32[]{:S(2)}) collective-permute-start(bf16[256,768]{1,0:T(8,128)(2,1)S(1)} %get-tuple-element.90), channel_id=1, source_target_pairs={{0,7},{1,6},{2,5},{3,4},{4,3},{5,2},{6,1},{7,0},{8,15},{9,14},{10,... | collective-permute-start | bytes 1179656 | tf_op jit(solution)/shard_map/ppermute | solution.py:51
  79.5 40.2 %collective-permute-start.5 = (bf16[256,256]{1,0:T(8,128)(2,1)S(1)}, bf16[256,256]{1,0:T(8,128)(2,1)S(1)}, u32[]{:S(2)}, u32[]{:S(2)}) collective-permute-start(bf16[256,256]{1,0:T(8,128)(2,1)S(1)} %get-tuple-element.73), channel_id=1, source_target_pairs={{0,4},{1,5},{2,6},{3,7},{4,0},{5,1},{6,2},{7,3},{8,12},{9,13},{10,... | collective-permute-start | bytes 393224 | tf_op jit(solution)/shard_map/ppermute | solution.py:51
  79.9 39.9 %collective-permute-start.13 = (bf16[256,256]{1,0:T(8,128)(2,1)S(1)}, bf16[256,256]{1,0:T(8,128)(2,1)S(1)}, u32[]{:S(2)}, u32[]{:S(2)}) collective-permute-start(bf16[256,256]{1,0:T(8,128)(2,1)S(1)} %get-tuple-element.83), channel_id=1, source_target_pairs={{0,6},{1,7},{2,4},{3,5},{4,2},{5,3},{6,0},{7,1},{8,14},{9,15},{10,... | collective-permute-start | bytes 393224 | tf_op jit(solution)/shard_map/ppermute | solution.py:51
  119.8 7.7 %collective-permute-start.20 = (f32[384,1024]{1,0:T(8,128)S(1)}, f32[384,1024]{1,0:T(8,128)S(1)}, u32[]{:S(2)}, u32[]{:S(2)}) collective-permute-start(f32[384,1024]{1,0:T(8,128)S(1)} %get-tuple-element.94), channel_id=1, source_target_pairs={{0,8},{8,0},{16,24},{24,16},{1,9},{9,1},{17,25},{25,17},{2,10},{10... | collective-permute-start | bytes 4718600 | tf_op jit(solution)/shard_map/ppermute | solution.py:333
  127.5 20.8 %copy-start.3 = (f32[1,1024,1024]{2,1,0:T(8,128)S(1)}, f32[1,1024,1024]{2,1,0:T(8,128)}, u32[]{:S(2)}) copy-start(f32[1,1024,1024]{2,1,0:T(8,128)} %refs_16_.3) | copy-start | bytes 12582916
  127.8 18.8 %collective-permute-start.21 = (f16[384,1024]{1,0:T(8,128)(2,1)S(1)}, f16[384,1024]{1,0:T(8,128)(2,1)S(1)}, u32[]{:S(2)}, u32[]{:S(2)}) collective-permute-start(f16[384,1024]{1,0:T(8,128)(2,1)S(1)} %add_convert_fusion), channel_id=1, source_target_pairs={{0,16},{8,24},{16,0},{24,8},{1,17},{9,25},{17,1},{25,9},{2,18},{10... | collective-permute-start | bytes 2359304 | tf_op jit(solution)/shard_map/ppermute | solution.py:337
  129.2 19.1 %collective-permute-start.10 = (bf16[256,256]{1,0:T(8,128)(2,1)S(1)}, bf16[256,256]{1,0:T(8,128)(2,1)S(1)}, u32[]{:S(2)}, u32[]{:S(2)}) collective-permute-start(bf16[256,256]{1,0:T(8,128)(2,1)S(1)} %get-tuple-element.79), channel_id=1, source_target_pairs={{0,5},{1,4},{2,7},{3,6},{4,1},{5,0},{6,3},{7,2},{8,13},{9,12},{10,... | collective-permute-start | bytes 393224 | tf_op jit(solution)/shard_map/ppermute | solution.py:51
  129.2 19.1 %collective-permute-start.14 = (bf16[256,256]{1,0:T(8,128)(2,1)S(1)}, bf16[256,256]{1,0:T(8,128)(2,1)S(1)}, u32[]{:S(2)}, u32[]{:S(2)}) collective-permute-start(bf16[256,256]{1,0:T(8,128)(2,1)S(1)} %get-tuple-element.85), channel_id=1, source_target_pairs={{0,7},{1,6},{2,5},{3,4},{4,3},{5,2},{6,1},{7,0},{8,15},{9,14},{10,... | collective-permute-start | bytes 393224 | tf_op jit(solution)/shard_map/ppermute | solution.py:51
  147.0 9.3 %collective-permute-start.22 = (f32[384,1024]{1,0:T(8,128)S(1)}, f32[384,1024]{1,0:T(8,128)S(1)}, u32[]{:S(2)}, u32[]{:S(2)}) collective-permute-start(f32[384,1024]{1,0:T(8,128)S(1)} %add_multiply_fusion.mine), channel_id=1, source_target_pairs={{0,8},{8,0},{16,24},{24,16},{1,9},{9,1},{17,25},{25,17},{2,10},{10... | collective-permute-start | bytes 4718600 | tf_op jit(solution)/shard_map/ppermute | solution.py:343
  152.8 2.0 %collective-permute-start.17 = (f32[128,1024]{1,0:T(8,128)S(1)}, f32[128,1024]{1,0:T(8,128)S(1)}, u32[]{:S(2)}, u32[]{:S(2)}) collective-permute-start(f32[128,1024]{1,0:T(8,128)S(1)} %get-tuple-element.88), channel_id=1, source_target_pairs={{0,8},{8,0},{16,24},{24,16},{1,9},{9,1},{17,25},{25,17},{2,10},{10... | collective-permute-start | bytes 1572872 | tf_op jit(solution)/shard_map/ppermute | solution.py:333
  154.8 7.8 %collective-permute-start.18 = (f16[128,1024]{1,0:T(8,128)(2,1)S(1)}, f16[128,1024]{1,0:T(8,128)(2,1)S(1)}, u32[]{:S(2)}, u32[]{:S(2)}) collective-permute-start(f16[128,1024]{1,0:T(8,128)(2,1)S(1)} %add_convert_fusion.1), channel_id=1, source_target_pairs={{0,16},{8,24},{16,0},{24,8},{1,17},{9,25},{17,1},{25,9},{2,18},{10... | collective-permute-start | bytes 786440 | tf_op jit(solution)/shard_map/ppermute | solution.py:337
  162.8 2.6 %collective-permute-start.23 = (f32[128,1024]{1,0:T(8,128)S(1)}, f32[128,1024]{1,0:T(8,128)S(1)}, u32[]{:S(2)}, u32[]{:S(2)}) collective-permute-start(f32[128,1024]{1,0:T(8,128)S(1)} %add_multiply_fusion.1.mine), channel_id=1, source_target_pairs={{0,8},{8,0},{16,24},{24,16},{1,9},{9,1},{17,25},{25,17},{2,10},{10... | collective-permute-start | bytes 1572872 | tf_op jit(solution)/shard_map/ppermute | solution.py:343

commit v2 on v1

v2 whole, which is shorter than its diff:
```python
import functools
import math

import jax
import jax.numpy as jnp
from jax import lax
from jax.experimental import pallas as pl
from jax.experimental.pallas import tpu as pltpu
from jax.sharding import PartitionSpec as P

beta_first = 0.8
beta_second = 0.9
inner_rate = 0.15
weight_decay = 0.1
adam_epsilon = 1e-08
outer_rate = 0.7
momentum_coef = 0.9
inner_count = 50

TILE = 128
VMEM = 40 * 1024 * 1024
SPLIT_VMEM = 60 * 1024 * 1024


ORDER = ("g2", "y0", "n0", "g1", "x00", "g3", "y1", "x01", "y2", "x03", "n1", "x02", "y3", "n2", "x10", "x11", "x12", "x13")
WINDOW = 5
SIZES = (6, 2)
SENT = (6, 2)
STEP_PINS = (("x10", "x11"),)
CORE_PINS = ((),)
CHIP_PINS = (("x12",),)
BLOCK = 256


def chunks_of(rows, sizes):
    units = rows // TILE
    if sum(sizes) != units:
        sizes = [units - len(sizes) + 1] + [1] * (len(sizes) - 1)
    result, at = [], 0
    for size in sizes:
        result.append((at, size * TILE))
        at += size * TILE
    return result


def pairs(n, k, keep=lambda i: True):
    return [(i, i ^ k) for i in range(n) if keep(i)]


def split_kernel(n, rows, pieces, info, x, *refs):
    outs, (buf, sem_in, sem_out) = refs[:-3], refs[-3:]
    reads, writes = [], []
    for k in range(n):
        start = pl.multiple_of((info[0] ^ k) * rows, TILE)
        reads.append(
            pltpu.make_async_copy(x.at[:, pl.ds(start, rows)], buf.at[k], sem_in.at[k])
        )
        reads[-1].start()
    for k in range(n):
        reads[k].wait()
        for j, (of, at, size) in enumerate(pieces):
            if of == k:
                copy = pltpu.make_async_copy(buf.at[k, :, pl.ds(at, size)], outs[j], sem_out.at[j])
                copy.start()
                writes.append(copy)
    for copy in writes:
        copy.wait()


def split_columns(info, x, n, rows, chunks):
    far = n // 2
    pieces = [(k, 0, rows) for k in range(far)]
    pieces += [(k, at, size) for at, size in chunks for k in range(far, n)]
    shapes = [jax.ShapeDtypeStruct((x.shape[0], size), x.dtype) for _, _, size in pieces]
    flat = pl.pallas_call(
        functools.partial(split_kernel, n, rows, pieces),
        in_specs=[pl.BlockSpec(memory_space=pltpu.SMEM), pl.BlockSpec(memory_space=pltpu.HBM)],
        out_specs=[pl.BlockSpec(memory_space=pltpu.HBM)] * len(shapes),
        scratch_shapes=[
            pltpu.VMEM((n, x.shape[0], rows), x.dtype),
            pltpu.SemaphoreType.DMA((n,)),
            pltpu.SemaphoreType.DMA((len(pieces),)),
        ],
        out_shape=shapes,
        compiler_params=pltpu.CompilerParams(vmem_limit_bytes=SPLIT_VMEM),
        name="split_columns",
    )(info, x)
    return flat[:far], [flat[far * (c + 1) : far * (c + 2)] for c in range(len(chunks))]


def exchange(block, whole, parts):
    n = lax.axis_size("fsdp")
    near, far = n // 4, n // 2
    gs = {0: block}
    xs = [{k: whole[k] for k in range(far)} for _ in parts]
    inside = [range(1, near), [near], range(near + 1, far)]
    crossing = [[far], [far + near], range(far + 1, far + near), range(far + near + 1, n)]
    arrived = {}
    for j, name in enumerate(ORDER):
        kind, which = name[0], int(name[1:])
        if kind == "g":
            jobs = [(which * near, gs[far] if which == 3 else block, near if which == 3 else which * near)]
        elif kind == "y":
            jobs = [(which * near + k, gs[which * near], k) for k in range(1, near)]
        elif kind == "n":
            jobs = [(k, whole[k], k) for k in inside[which]]
        else:
            jobs = [(k, parts[which // 10][k - far], k) for k in crossing[which % 10]]
        after = arrived[ORDER[j - WINDOW]] if j >= WINDOW else []
        if name in ("y1", "g3"):
            after = [after, whole, parts]
        arrived[name] = []
        for key, value, k in jobs:
            if after:
                value, _ = lax.optimization_barrier((value, after))
            moved = lax.ppermute(value, "fsdp", pairs(n, k))
            arrived[name].append(moved)
            if kind in "gy":
                gs[key] = moved
            elif kind == "n":
                for x in xs:
                    x[key] = moved
            else:
                xs[which // 10][key] = moved
    return [gs[k] for k in range(n)], [[x[k] for k in range(n)] for x in xs], arrived


def step_kernel(n, at, share, scale, info, *refs):
    xs, gs = refs[:n], refs[n : 2 * n]
    params, first, second, anchor, momentum, send, keep = refs[2 * n :]
    gradient = None
    for x, g in zip(xs, gs):
        term = lax.dot_general(
            x[...], g[...], (((0,), (0,)), ((), ())), preferred_element_type=jnp.float32
        )
        gradient = term if gradient is None else gradient + term
    moment_one = beta_first * first[0] + (1.0 - beta_first) * gradient
    moment_two = beta_second * second[0] + (1.0 - beta_second) * gradient * gradient
    first_correction = 1.0 - beta_first**inner_count
    second_correction = 1.0 - beta_second**inner_count
    ratio = (
        moment_one
        * (1.0 / first_correction)
        / (jnp.sqrt(moment_two * (1.0 / second_correction)) + adam_epsilon)
    )
    stepped = params[0] - inner_rate * (ratio + weight_decay * params[0])
    core, worker = info[1], info[2]
    half = stepped.shape[1] // 2
    block = stepped.shape[0]
    piece = min(share, block)
    offset = worker * share - (at + pl.program_id(0) * block)
    inside = (offset > -share) & (offset < block)

    def store(left, right):
        left[...] = stepped[:, :half]
        right[...] = stepped[:, half:]

        @pl.when(inside)
        def _():
            rows = pl.ds(pl.multiple_of(jnp.maximum(offset, 0), piece), piece)
            term = owner_term(anchor[...], momentum[...], scale)
            left[rows] += term[:, :half]
            right[rows] += term[:, half:]

    pl.when(core == 0)(lambda: store(keep, send))
    pl.when(core != 0)(lambda: store(send, keep))


def owner_term(anchor, momentum, scale):
    step = outer_rate * (1.0 + momentum_coef)
    return (scale * (1.0 - step) / step) * anchor - (
        scale * outer_rate * momentum_coef**2 / step
    ) * momentum


def inner_step(info, xs, gs, params, first, second, anchor, momentum, scale, at, size):
    n = len(gs)
    tokens, width = gs[0].shape
    share = anchor.shape[0]
    block = math.gcd(size, BLOCK)
    piece = min(share, block)

    def owned(i, info):
        ahead = at + i * block - info[2] * share
        return (jnp.clip(ahead // piece, 0, share // piece - 1), 0)

    columns = [
        pl.BlockSpec(
            (pl.Element(tokens), pl.Element(block)),
            lambda i, info, skip=at - start: (0, pl.multiple_of(skip + i * block, TILE)),
        )
        for _, start in xs
    ]
    whole = pl.BlockSpec((tokens, width), lambda i, info: (0, 0))
    state = pl.BlockSpec((pl.Element(1), pl.Element(block), pl.Element(width)), lambda i, info: (0, pl.multiple_of(at + i * block, TILE), 0))
    part = pl.BlockSpec((block, width // 2), lambda i, info: (i, 0))
    shape = jax.ShapeDtypeStruct((size, width // 2), jnp.float32)
    return pl.pallas_call(
        functools.partial(step_kernel, n, at, share, scale),
        grid_spec=pltpu.PrefetchScalarGridSpec(
            num_scalar_prefetch=1,
            grid=(size // block,),
            in_specs=columns
            + [whole] * n
            + [state] * 3
            + [pl.BlockSpec((piece, width), owned)] * 2,
            out_specs=[part, part],
        ),
        out_shape=[shape, shape],
        compiler_params=pltpu.CompilerParams(vmem_limit_bytes=VMEM),
        name="inner_step",
    )(info, *[x for x, _ in xs], *gs, params, first, second, anchor, momentum)


def outer_kernel(at, share, info, mine, other, anchor, momentum, *refs):
    whole, fresh, buf, sem, sem_fresh = refs[-5:]
    core, worker = info[1], info[2]
    size, half = mine.shape
    copies = []
    for j, (source, side) in enumerate(((mine, core), (other, 1 - core))):
        columns = pl.ds(pl.multiple_of(side * half, half), half)
        copies.append(
            pltpu.make_async_copy(source, whole.at[pl.ds(at, size), columns], sem.at[j])
        )
        copies[-1].start()
    step = outer_rate * (1.0 + momentum_coef)
    piece = min(share, TILE)
    for p in range(share // piece):
        row = worker * share + p * piece - at
        part = pl.ds(p * piece, piece)

        @pl.when((row >= 0) & (row < size))
        def _(row=row, part=part, p=p):
            rows = pl.ds(pl.multiple_of(row, piece), piece)

            def write(left, right):
                base = (momentum_coef - outer_rate * momentum_coef**2 / step) * momentum[part] + (
                    1.0 + (1.0 - step) / step
                ) * anchor[part]
                buf[part, :half] = base[:, :half] - (1.0 / step) * left[rows]
                buf[part, half:] = base[:, half:] - (1.0 / step) * right[rows]

            pl.when(core == 0)(lambda: write(mine, other))
            pl.when(core != 0)(lambda: write(other, mine))
            copy = pltpu.make_async_copy(buf.at[part], fresh.at[part], sem_fresh.at[p])
            copy.start()
            copy.wait()

    for copy in copies:
        copy.wait()


def outer_step(info, mine, other, anchor, momentum, state, rows, at):
    share, width = anchor.shape
    shapes = [
        jax.ShapeDtypeStruct((rows, width), jnp.float32),
        jax.ShapeDtypeStruct((share, width), jnp.float32),
    ]
    return pl.pallas_call(
        functools.partial(outer_kernel, at, share),
        in_specs=[pl.BlockSpec(memory_space=pltpu.SMEM)]
        + [pl.BlockSpec(memory_space=pltpu.VMEM)] * 4
        + [pl.BlockSpec(memory_space=pl.ANY)] * len(state),
        out_specs=[pl.BlockSpec(memory_space=pl.ANY)] * 2,
        out_shape=shapes,
        scratch_shapes=[
            pltpu.VMEM((share, width), jnp.float32),
            pltpu.SemaphoreType.DMA((2,)),
            pltpu.SemaphoreType.DMA((share // min(share, TILE),)),
        ],
        input_output_aliases={5: 0, 6: 1} if state else {},
        compiler_params=pltpu.CompilerParams(vmem_limit_bytes=VMEM),
        name="outer_step",
    )(info, mine, other, anchor, momentum, *state)


def shards(
    inputs, output_grads, local_params, first_moment, second_moment, global_params, momentum
):
    n, replicas = lax.axis_size("fsdp"), lax.axis_size("worker")
    me, worker = lax.axis_index("fsdp"), lax.axis_index("worker")
    info = jnp.stack([me, worker % 2, worker]).astype(jnp.int32)
    features = inputs[0]
    rows = local_params.shape[1]
    chunks = chunks_of(rows, SIZES)
    sent = chunks_of(rows, SENT)
    step = outer_rate * (1.0 + momentum_coef)

    own, parts = split_columns(info, features, n, rows, sent)
    gs, columns, arrived = exchange(output_grads[0], own, parts)
    state, waiting = [], ()
    for c, (at, size) in enumerate(chunks):
        part = max(j for j, (start, _) in enumerate(sent) if start <= at)
        xs = [(x, 0 if k < n // 2 else sent[part][0]) for k, x in enumerate(columns[part])]
        send, keep = inner_step(
            info,
            xs,
            gs,
            local_params,
            first_moment,
            second_moment,
            global_params,
            momentum,
            float(replicas),
            at,
            size,
        )
        pins = [
            [arrived[name] for name in table[c]] if c + 1 < len(chunks) else []
            for table in (STEP_PINS, CORE_PINS, CHIP_PINS)
        ]
        send, keep, _ = lax.optimization_barrier((send, keep, pins[0]))
        got = lax.ppermute(send, "worker", pairs(replicas, 1))
        got, _ = lax.optimization_barrier((got, pins[1]))
        total = keep + got
        k = 2
        while k < replicas:
            half = total.astype(jnp.float16)
            if k == 2 and waiting:
                if state:
                    half, state = lax.optimization_barrier((half, state))
                state = outer_step(info, *waiting, global_params, momentum, state, rows, chunks[c - 1][0])
            got = lax.ppermute(half, "worker", pairs(replicas, k))
            if k == 2:
                got, _ = lax.optimization_barrier((got, pins[2]))
            total = half.astype(jnp.float32) + got.astype(jnp.float32)
            k *= 2
        mine = total * (step / replicas)
        other = lax.ppermute(mine, "worker", pairs(replicas, 1))
        waiting = (mine, other)
    return tuple(outer_step(info, *waiting, global_params, momentum, state, rows, at))


def solution(mesh):
    return jax.shard_map(
        shards,
        mesh=mesh,
        in_specs=(
            P("worker", "fsdp", None),
            P("worker", "fsdp", None),
            P("worker", "fsdp", None),
            P("worker", "fsdp", None),
            P("worker", "fsdp", None),
            P(("fsdp", "worker"), None),
            P(("fsdp", "worker"), None),
        ),
        out_specs=(P("fsdp", None), P(("fsdp", "worker"), None)),
        check_vma=False,
    )
```

time: 168 us -> 159 us (0.946)
  waiting for transfers between devices: 111 us -> 103 us
  Pallas kernels: 20.7 us -> 23.8 us
  starting transfers between devices: 30.9 us -> 28.9 us
    ppermute x2, waiting for transfers between devices: 19.1 us -> 7.11 us  [shards(): got = lax.ppermute(half, 'worker', pairs(replicas, k))]
    ppermute x20, waiting for transfers between devices: 90.7 us -> 95.6 us  [the longest x18 91.7 us: exchange(): moved = lax.ppermute(value, 'fsdp', pairs(n, k))]
    pallas_call x1, Pallas kernels: 1.49 us -> 4.47 us  [split_columns(): pl.pallas_call(functools.partial(split_kernel, n, rows, pieces), in_specs...]
  transfers between devices with their start and end apart: 24 -> 24, of which waited for: 12 -> 12; matrix products, arithmetic and copies ran while one was open for 0% -> 1% of each run, Pallas kernels for 11% -> 14%
where the time goes in v2:
time: 159 us
  waiting for transfers between devices  103 us (65%)
  starting transfers between devices  28.9 us (18%)
  Pallas kernels  23.8 us (15%)
    ppermute x18, waiting for transfers between devices, exchange(): moved = lax.ppermute(value, 'fsdp', pairs(n, k))  91.7 us
    ppermute x18, starting transfers between devices, exchange(): moved = lax.ppermute(value, 'fsdp', pairs(n, k))  18.8 us
    pallas_call x2, Pallas kernels, inner_step(): pl.pallas_call(functools.partial(step_kernel, n, at, share, scale), grid_...  14.4 us
    ppermute x2, waiting for transfers between devices, shards(): got = lax.ppermute(half, 'worker', pairs(replicas, k))  7.11 us
    ppermute x2, starting transfers between devices, shards(): got = lax.ppermute(send, 'worker', pairs(replicas, 1))  6.66 us
    pallas_call x2, Pallas kernels, outer_step(): pl.pallas_call(functools.partial(outer_kernel, at, share), in_specs=[pl.B...  4.89 us
    pallas_call x1, Pallas kernels, split_columns(): pl.pallas_call(functools.partial(split_kernel, n, rows, pieces), in_specs...  4.47 us
    ppermute x2, waiting for transfers between devices, shards(): got = lax.ppermute(send, 'worker', pairs(replicas, 1))  3.88 us
  transfers between devices with their start and end apart: 24, of which 12 were waited for; matrix products, arithmetic and copies ran while one was open for 1% of the time, Pallas kernels for 14%

profile of v2, /device:TPU:9, one launch (start us, length us, event | category | flops | bytes accessed | tf_op | source)
XLA Modules:
  0.0 158.7 jit_solution(7417153168368551873)
XLA Ops:
  0.6 2.4 %collective-permute-start.1 = (bf16[256,1024]{1,0:T(8,128)(2,1)}, bf16[256,1024]{1,0:T(8,128)(2,1)S(1)}, u32[]{:S(2)}, u32[]{:S(2)}) collective-permute-start(bf16[256,1024]{1,0:T(8,128)(2,1)} %bitcast.5), channel_id=1, source_target_pairs={{0,4},{1,5},{2,6},{3,7},{4,0},{5,1},{6,2},{7,3},{8,12},{9,13},{10,... | collective-permute-start | bytes 1572872 | tf_op jit(solution)/shard_map/ppermute | solution.py:116
  3.0 0.2 collective-permute-start.4
  3.2 1.2 collective-permute-start.10
  4.4 0.6 pad_add_fusion.info
  5.0 4.5 %split_columns.1 = (bf16[256,1024]{1,0:T(8,128)(2,1)}, bf16[256,1024]{1,0:T(8,128)(2,1)}, bf16[256,1024]{1,0:T(8,128)(2,1)}, bf16[256,1024]{1,0:T(8,128)(2,1)}, ...) custom-call(s32[3]{0:T(128)} %pad_add_fusion.info, ...), custom_call_target="tpu_custom_call" | custom-call | tf_op jit(solution)/shard_map/split_columns/pallas_call | solution.py:75
  9.5 0.3 collective-permute-start
  9.8 16.3 %collective-permute-done.1.refs_12_ = bf16[256,1024]{1,0:T(8,128)(2,1)S(1)} collective-permute-done((bf16[256,1024]{1,0:T(8,128)(2,1)}, bf16[256,1024]{1,0:T(8,128)(2,1)S(1)}, u32[]{:S(2)}, u32[]{:S(2)}) %collective-permute-start.1) | collective-permute-done | bytes 524320 | tf_op jit(solution)/shard_map/ppermute | solution.py:116
  26.1 0.2 collective-permute-start.2
  26.3 0.0 collective-permute-done.4.refs_10_
  26.3 1.0 collective-permute-start.5
  27.3 3.0 %collective-permute-start.7 = (bf16[256,768]{1,0:T(8,128)(2,1)}, bf16[256,768]{1,0:T(8,128)(2,1)S(1)}, u32[]{:S(2)}, u32[]{:S(2)}) collective-permute-start(bf16[256,768]{1,0:T(8,128)(2,1)} %get-tuple-element.40), channel_id=1, source_target_pairs={{0,4},{1,5},{2,6},{3,7},{4,0},{5,1},{6,2},{7,3},{8,12},{9,13},{10,... | collective-permute-start | bytes 1179656 | tf_op jit(solution)/shard_map/ppermute | solution.py:116
  30.3 0.2 collective-permute-start.11
  30.6 0.0 collective-permute-done.refs_1_
  30.6 0.3 collective-permute-start.15
  30.8 13.8 %collective-permute-done.2.refs_14_ = bf16[256,1024]{1,0:T(8,128)(2,1)S(1)} collective-permute-done((bf16[256,1024]{1,0:T(8,128)(2,1)S(1)}, bf16[256,1024]{1,0:T(8,128)(2,1)S(1)}, u32[]{:S(2)}, u32[]{:S(2)}) %collective-permute-start.2) | collective-permute-done | bytes 524320 | tf_op jit(solution)/shard_map/ppermute | solution.py:116
  44.6 2.2 %collective-permute-start.3 = (bf16[256,1024]{1,0:T(8,128)(2,1)}, bf16[256,1024]{1,0:T(8,128)(2,1)S(1)}, u32[]{:S(2)}, u32[]{:S(2)}) collective-permute-start(bf16[256,1024]{1,0:T(8,128)(2,1)} %get-tuple-element.49), channel_id=1, source_target_pairs={{0,2},{1,3},{2,0},{3,1},{4,6},{5,7},{6,4},{7,5},{8,10},{9,11},{10,... | collective-permute-start | bytes 1572872 | tf_op jit(solution)/shard_map/ppermute | solution.py:116
  46.8 2.6 %collective-permute-done.7.refs_4_ = bf16[256,768]{1,0:T(8,128)(2,1)S(1)} collective-permute-done((bf16[256,768]{1,0:T(8,128)(2,1)}, bf16[256,768]{1,0:T(8,128)(2,1)S(1)}, u32[]{:S(2)}, u32[]{:S(2)}) %collective-permute-start.7) | collective-permute-done | bytes 393248 | tf_op jit(solution)/shard_map/ppermute | solution.py:116
  49.4 2.5 %collective-permute-start.8 = (bf16[256,768]{1,0:T(8,128)(2,1)}, bf16[256,768]{1,0:T(8,128)(2,1)S(1)}, u32[]{:S(2)}, u32[]{:S(2)}) collective-permute-start(bf16[256,768]{1,0:T(8,128)(2,1)} %get-tuple-element.52), channel_id=1, source_target_pairs={{0,7},{1,6},{2,5},{3,4},{4,3},{5,2},{6,1},{7,0},{8,15},{9,14},{10,... | collective-permute-start | bytes 1179656 | tf_op jit(solution)/shard_map/ppermute | solution.py:116
  51.9 12.7 %collective-permute-done.15.refs_6_ = bf16[256,768]{1,0:T(8,128)(2,1)S(1)} collective-permute-done((bf16[256,768]{1,0:T(8,128)(2,1)}, bf16[256,768]{1,0:T(8,128)(2,1)S(1)}, u32[]{:S(2)}, u32[]{:S(2)}) %collective-permute-start.15) | collective-permute-done | bytes 393248 | tf_op jit(solution)/shard_map/ppermute | solution.py:116
  64.6 0.2 collective-permute-start.16
  64.8 0.0 collective-permute-start.12
  64.8 18.6 %collective-permute-done.8.refs_7_ = bf16[256,768]{1,0:T(8,128)(2,1)S(1)} collective-permute-done((bf16[256,768]{1,0:T(8,128)(2,1)}, bf16[256,768]{1,0:T(8,128)(2,1)S(1)}, u32[]{:S(2)}, u32[]{:S(2)}) %collective-permute-start.8) | collective-permute-done | bytes 393248 | tf_op jit(solution)/shard_map/ppermute | solution.py:116
  83.5 1.1 collective-permute-start.14
  84.6 12.8 %collective-permute-done.12.refs_5_ = bf16[256,768]{1,0:T(8,128)(2,1)S(1)} collective-permute-done((bf16[256,768]{1,0:T(8,128)(2,1)}, bf16[256,768]{1,0:T(8,128)(2,1)S(1)}, u32[]{:S(2)}, u32[]{:S(2)}) %collective-permute-start.12) | collective-permute-done | bytes 393248 | tf_op jit(solution)/shard_map/ppermute | solution.py:116
  97.4 0.0 collective-permute-done.6.refs_3_
  97.4 5.4 %collective-permute-done.16.refs_15_ = bf16[256,1024]{1,0:T(8,128)(2,1)S(1)} collective-permute-done((bf16[256,1024]{1,0:T(8,128)(2,1)S(1)}, bf16[256,1024]{1,0:T(8,128)(2,1)S(1)}, u32[]{:S(2)}, u32[]{:S(2)}) %collective-permute-start.16) | collective-permute-done | bytes 524320 | tf_op jit(solution)/shard_map/ppermute | solution.py:116
  102.8 0.0 copy-start.4
  102.8 1.0 copy-done.4
  103.8 10.0 %inner_step.3 = (f32[768,512]{1,0:T(8,128)S(1)}, f32[768,512]{1,0:T(8,128)S(1)}) custom-call(s32[3]{0:T(128)S(1)} %copy-done.5, bf16[256,1024]{1,0:T(8,128)(2,1)S(1)} %copy-done.4, bf16[256,1024]{1,0:T(8,128)(2,1)S(1)} %collective-permute-done.refs_1_, bf16[256,1024]{1,0:T(8,128)(2,1)S(1)} %collective-permute-done.3.refs_2_, ...), custom_call_target="tpu_custom_call" | custom-call | tf_op jit(solution)/shard_map/inner_step/pallas_call | solution.py:198
  113.9 6.1 %collective-permute-start.21 = (f32[768,512]{1,0:T(8,128)S(1)}, f32[768,512]{1,0:T(8,128)S(1)}, u32[]{:S(2)}, u32[]{:S(2)}) collective-permute-start(f32[768,512]{1,0:T(8,128)S(1)} %get-tuple-element.66), channel_id=1, source_target_pairs={{0,8},{8,0},{16,24},{24,16},{1,9},{9,1},{17,25},{25,17},{2,10},{10... | collective-permute-start | bytes 4718600 | tf_op jit(solution)/shard_map/ppermute | solution.py:313
  120.0 3.0 %collective-permute-done.21 = f32[768,512]{1,0:T(8,128)S(1)} collective-permute-done((f32[768,512]{1,0:T(8,128)S(1)}, f32[768,512]{1,0:T(8,128)S(1)}, u32[]{:S(2)}, u32[]{:S(2)}) %collective-permute-start.21) | collective-permute-done | bytes 1572896 | tf_op jit(solution)/shard_map/ppermute | solution.py:313
  123.0 0.4 add_convert_fusion
  123.4 1.3 collective-permute-start.22
  124.7 3.9 %collective-permute-start.13 = (bf16[256,256]{1,0:T(8,128)(2,1)S(1)}, bf16[256,256]{1,0:T(8,128)(2,1)S(1)}, u32[]{:S(2)}, u32[]{:S(2)}) collective-permute-start(bf16[256,256]{1,0:T(8,128)(2,1)S(1)} %copy-done.7), channel_id=1, source_target_pairs={{0,5},{1,4},{2,7},{3,6},{4,1},{5,0},{6,3},{7,2},{8,13},{9,12},{10,... | collective-permute-start | bytes 393224 | tf_op jit(solution)/shard_map/ppermute | solution.py:116
  128.6 4.9 %collective-permute-done.13.refs_5_ = bf16[256,256]{1,0:T(8,128)(2,1)S(1)} collective-permute-done((bf16[256,256]{1,0:T(8,128)(2,1)S(1)}, bf16[256,256]{1,0:T(8,128)(2,1)S(1)}, u32[]{:S(2)}, u32[]{:S(2)}) %collective-permute-start.13) | collective-permute-done | bytes 131104 | tf_op jit(solution)/shard_map/ppermute | solution.py:116
  133.5 4.7 %collective-permute-done.17.refs_7_ = bf16[256,256]{1,0:T(8,128)(2,1)S(1)} collective-permute-done((bf16[256,256]{1,0:T(8,128)(2,1)S(1)}, bf16[256,256]{1,0:T(8,128)(2,1)S(1)}, u32[]{:S(2)}, u32[]{:S(2)}) %collective-permute-start.17) | collective-permute-done | bytes 131104 | tf_op jit(solution)/shard_map/ppermute | solution.py:116
  138.2 4.4 %inner_step.2 = (f32[256,512]{1,0:T(8,128)S(1)}, f32[256,512]{1,0:T(8,128)S(1)}) custom-call(s32[3]{0:T(128)S(1)} %copy-done.5, bf16[256,1024]{1,0:T(8,128)(2,1)S(1)} %copy-done.4, bf16[256,1024]{1,0:T(8,128)(2,1)S(1)} %collective-permute-done.refs_1_, bf16[256,1024]{1,0:T(8,128)(2,1)S(1)} %collective-permute-done.3.refs_2_, ...), custom_call_target="tpu_custom_call" | custom-call | tf_op jit(solution)/shard_map/inner_step/pallas_call | solution.py:198
  142.6 0.5 collective-permute-start.18
  143.1 0.3 add_multiply_fusion.mine
  143.4 0.4 collective-permute-start.23
  143.8 0.8 collective-permute-done.18
  144.7 0.1 add_convert_fusion.1
  144.8 0.5 collective-permute-start.19
  145.3 7.1 %collective-permute-done.19 = f16[256,512]{1,0:T(8,128)(2,1)S(1)} collective-permute-done((f16[256,512]{1,0:T(8,128)(2,1)S(1)}, f16[256,512]{1,0:T(8,128)(2,1)S(1)}, u32[]{:S(2)}, u32[]{:S(2)}) %collective-permute-start.19) | collective-permute-done | bytes 262176 | tf_op jit(solution)/shard_map/ppermute | solution.py:323
  152.4 0.1 add_multiply_fusion.1.mine
  152.5 1.3 collective-permute-start.20
  153.8 3.3 %outer_step.2 = (f32[1024,1024]{1,0:T(8,128)}, f32[256,1024]{1,0:T(8,128)}) custom-call(s32[3]{0:T(128)S(1)} %copy-done.5, f32[768,512]{1,0:T(8,128)S(1)} %add_multiply_fusion.mine, f32[768,512]{1,0:T(8,128)S(1)} %collective-permute-done.23.other, f32[256,1024]{1,0:T(8,128)S(1)} %copy-done, f32[256,1024]{1,0:T(8,128)S(1)} %copy-done.1), custom_call_target="tpu_custom_call" | custom-call | tf_op jit(solution)/shard_map/outer_step/pallas_call | solution.py:259
  157.1 1.5 outer_step.3
  (26 shorter events, 0.1 us)
Async XLA Ops:
  0.6 25.5 %collective-permute-start.1 = (bf16[256,1024]{1,0:T(8,128)(2,1)}, bf16[256,1024]{1,0:T(8,128)(2,1)S(1)}, u32[]{:S(2)}, u32[]{:S(2)}) collective-permute-start(bf16[256,1024]{1,0:T(8,128)(2,1)} %bitcast.5), channel_id=1, source_target_pairs={{0,4},{1,5},{2,6},{3,7},{4,0},{5,1},{6,2},{7,3},{8,12},{9,13},{10,... | collective-permute-start | bytes 1572872 | tf_op jit(solution)/shard_map/ppermute | solution.py:116
  3.0 23.3 %collective-permute-start.4 = (bf16[256,1024]{1,0:T(8,128)(2,1)}, bf16[256,1024]{1,0:T(8,128)(2,1)S(1)}, u32[]{:S(2)}, u32[]{:S(2)}) collective-permute-start(bf16[256,1024]{1,0:T(8,128)(2,1)} %bitcast.6), channel_id=1, source_target_pairs={{0,2},{1,3},{2,0},{3,1},{4,6},{5,7},{6,4},{7,5},{8,10},{9,11},{10,... | collective-permute-start | bytes 1572872 | tf_op jit(solution)/shard_map/ppermute | solution.py:116
  3.2 27.2 %collective-permute-start.10 = (bf16[256,1024]{1,0:T(8,128)(2,1)}, bf16[256,1024]{1,0:T(8,128)(2,1)}, u32[]{:S(2)}, u32[]{:S(2)}) collective-permute-start(bf16[256,1024]{1,0:T(8,128)(2,1)} %bitcast.7), channel_id=1, source_target_pairs={{0,1},{1,0},{2,3},{3,2},{4,5},{5,4},{6,7},{7,6},{8,9},{9,8},{10,11... | collective-permute-start | bytes 1572872 | tf_op jit(solution)/shard_map/ppermute | solution.py:116
  5.0 97.8 %copy-start = (f32[256,1024]{1,0:T(8,128)S(1)}, f32[256,1024]{1,0:T(8,128)}, u32[]{:S(2)}) copy-start(f32[256,1024]{1,0:T(8,128)} %anchor.3) | copy-start | bytes 3145732
  5.0 97.8 %copy-start.1 = (f32[256,1024]{1,0:T(8,128)S(1)}, f32[256,1024]{1,0:T(8,128)}, u32[]{:S(2)}) copy-start(f32[256,1024]{1,0:T(8,128)} %momentum.3) | copy-start | bytes 3145732
  5.0 97.8 %copy-start.3 = (bf16[1,256,1024]{2,1,0:T(8,128)(2,1)S(1)}, bf16[1,256,1024]{2,1,0:T(8,128)(2,1)}, u32[]{:S(2)}) copy-start(bf16[1,256,1024]{2,1,0:T(8,128)(2,1)} %param.8) | copy-start | bytes 1572868
  5.0 97.8 %copy-start.5 = (s32[3]{0:T(128)S(1)}, s32[3]{0:T(128)}, u32[]{:S(2)}) copy-start(s32[3]{0:T(128)} %pad_add_fusion.info) | copy-start | bytes 40
  9.5 21.1 %collective-permute-start = (bf16[256,1024]{1,0:T(8,128)(2,1)}, bf16[256,1024]{1,0:T(8,128)(2,1)S(1)}, u32[]{:S(2)}, u32[]{:S(2)}) collective-permute-start(bf16[256,1024]{1,0:T(8,128)(2,1)} %get-tuple-element.37), channel_id=1, source_target_pairs={{0,1},{1,0},{2,3},{3,2},{4,5},{5,4},{6,7},{7,6},{8,9},{9,8},{10,11... | collective-permute-start | bytes 1572872 | tf_op jit(solution)/shard_map/ppermute | solution.py:116
  26.1 18.5 %collective-permute-start.2 = (bf16[256,1024]{1,0:T(8,128)(2,1)S(1)}, bf16[256,1024]{1,0:T(8,128)(2,1)S(1)}, u32[]{:S(2)}, u32[]{:S(2)}) collective-permute-start(bf16[256,1024]{1,0:T(8,128)(2,1)S(1)} %collective-permute-done.1.refs_12_), channel_id=1, source_target_pairs={{0,2},{1,3},{2,0},{3,1},{4,6},{5,7},{6,4},{7,5},{8,10},{9,11},{10,... | collective-permute-start | bytes 1572872 | tf_op jit(solution)/shard_map/ppermute | solution.py:116
  26.3 25.6 %collective-permute-start.5 = (bf16[256,1024]{1,0:T(8,128)(2,1)S(1)}, bf16[256,1024]{1,0:T(8,128)(2,1)S(1)}, u32[]{:S(2)}, u32[]{:S(2)}) collective-permute-start(bf16[256,1024]{1,0:T(8,128)(2,1)S(1)} %collective-permute-done.1.refs_12_), channel_id=1, source_target_pairs={{0,1},{1,0},{2,3},{3,2},{4,5},{5,4},{6,7},{7,6},{8,9},{9,8},{10,11... | collective-permute-start | bytes 1572872 | tf_op jit(solution)/shard_map/ppermute | solution.py:116
  27.3 22.1 %collective-permute-start.7 = (bf16[256,768]{1,0:T(8,128)(2,1)}, bf16[256,768]{1,0:T(8,128)(2,1)S(1)}, u32[]{:S(2)}, u32[]{:S(2)}) collective-permute-start(bf16[256,768]{1,0:T(8,128)(2,1)} %get-tuple-element.40), channel_id=1, source_target_pairs={{0,4},{1,5},{2,6},{3,7},{4,0},{5,1},{6,2},{7,3},{8,12},{9,13},{10,... | collective-permute-start | bytes 1179656 | tf_op jit(solution)/shard_map/ppermute | solution.py:116
  30.3 34.5 %collective-permute-start.11 = (bf16[256,1024]{1,0:T(8,128)(2,1)S(1)}, bf16[256,1024]{1,0:T(8,128)(2,1)S(1)}, u32[]{:S(2)}, u32[]{:S(2)}) collective-permute-start(bf16[256,1024]{1,0:T(8,128)(2,1)S(1)} %collective-permute-done.4.refs_10_), channel_id=1, source_target_pairs={{0,1},{1,0},{2,3},{3,2},{4,5},{5,4},{6,7},{7,6},{8,9},{9,8},{10,11... | collective-permute-start | bytes 1572872 | tf_op jit(solution)/shard_map/ppermute | solution.py:116
  30.6 34.1 %collective-permute-start.15 = (bf16[256,768]{1,0:T(8,128)(2,1)}, bf16[256,768]{1,0:T(8,128)(2,1)S(1)}, u32[]{:S(2)}, u32[]{:S(2)}) collective-permute-start(bf16[256,768]{1,0:T(8,128)(2,1)} %get-tuple-element.58), channel_id=1, source_target_pairs={{0,6},{1,7},{2,4},{3,5},{4,2},{5,3},{6,0},{7,1},{8,14},{9,15},{10,... | collective-permute-start | bytes 1179656 | tf_op jit(solution)/shard_map/ppermute | solution.py:116
  44.6 38.8 %collective-permute-start.3 = (bf16[256,1024]{1,0:T(8,128)(2,1)}, bf16[256,1024]{1,0:T(8,128)(2,1)S(1)}, u32[]{:S(2)}, u32[]{:S(2)}) collective-permute-start(bf16[256,1024]{1,0:T(8,128)(2,1)} %get-tuple-element.49), channel_id=1, source_target_pairs={{0,2},{1,3},{2,0},{3,1},{4,6},{5,7},{6,4},{7,5},{8,10},{9,11},{10,... | collective-permute-start | bytes 1572872 | tf_op jit(solution)/shard_map/ppermute | solution.py:116
  49.4 34.0 %collective-permute-start.8 = (bf16[256,768]{1,0:T(8,128)(2,1)}, bf16[256,768]{1,0:T(8,128)(2,1)S(1)}, u32[]{:S(2)}, u32[]{:S(2)}) collective-permute-start(bf16[256,768]{1,0:T(8,128)(2,1)} %get-tuple-element.52), channel_id=1, source_target_pairs={{0,7},{1,6},{2,5},{3,4},{4,3},{5,2},{6,1},{7,0},{8,15},{9,14},{10,... | collective-permute-start | bytes 1179656 | tf_op jit(solution)/shard_map/ppermute | solution.py:116
  51.9 45.4 %collective-permute-start.6 = (bf16[256,1024]{1,0:T(8,128)(2,1)}, bf16[256,1024]{1,0:T(8,128)(2,1)S(1)}, u32[]{:S(2)}, u32[]{:S(2)}) collective-permute-start(bf16[256,1024]{1,0:T(8,128)(2,1)} %get-tuple-element.51), channel_id=1, source_target_pairs={{0,3},{1,2},{2,1},{3,0},{4,7},{5,6},{6,5},{7,4},{8,11},{9,10},{10,... | collective-permute-start | bytes 1572872 | tf_op jit(solution)/shard_map/ppermute | solution.py:116
  64.6 38.1 %collective-permute-start.16 = (bf16[256,1024]{1,0:T(8,128)(2,1)S(1)}, bf16[256,1024]{1,0:T(8,128)(2,1)S(1)}, u32[]{:S(2)}, u32[]{:S(2)}) collective-permute-start(bf16[256,1024]{1,0:T(8,128)(2,1)S(1)} %collective-permute-done.2.refs_14_), channel_id=1, source_target_pairs={{0,1},{1,0},{2,3},{3,2},{4,5},{5,4},{6,7},{7,6},{8,9},{9,8},{10,11... | collective-permute-start | bytes 1572872 | tf_op jit(solution)/shard_map/ppermute | solution.py:116
  64.8 32.6 %collective-permute-start.12 = (bf16[256,768]{1,0:T(8,128)(2,1)}, bf16[256,768]{1,0:T(8,128)(2,1)S(1)}, u32[]{:S(2)}, u32[]{:S(2)}) collective-permute-start(bf16[256,768]{1,0:T(8,128)(2,1)} %get-tuple-element.55), channel_id=1, source_target_pairs={{0,5},{1,4},{2,7},{3,6},{4,1},{5,0},{6,3},{7,2},{8,13},{9,12},{10,... | collective-permute-start | bytes 1179656 | tf_op jit(solution)/shard_map/ppermute | solution.py:116
  83.4 30.4 %collective-permute-start.9 = (bf16[256,256]{1,0:T(8,128)(2,1)}, bf16[256,256]{1,0:T(8,128)(2,1)S(1)}, u32[]{:S(2)}, u32[]{:S(2)}) collective-permute-start(bf16[256,256]{1,0:T(8,128)(2,1)} %get-tuple-element.53), channel_id=1, source_target_pairs={{0,4},{1,5},{2,6},{3,7},{4,0},{5,1},{6,2},{7,3},{8,12},{9,13},{10,... | collective-permute-start | bytes 393224 | tf_op jit(solution)/shard_map/ppermute | solution.py:116
  83.5 30.4 %collective-permute-start.14 = (bf16[256,256]{1,0:T(8,128)(2,1)}, bf16[256,256]{1,0:T(8,128)(2,1)S(1)}, u32[]{:S(2)}, u32[]{:S(2)}) collective-permute-start(bf16[256,256]{1,0:T(8,128)(2,1)} %get-tuple-element.57), channel_id=1, source_target_pairs={{0,6},{1,7},{2,4},{3,5},{4,2},{5,3},{6,0},{7,1},{8,14},{9,15},{10,... | collective-permute-start | bytes 393224 | tf_op jit(solution)/shard_map/ppermute | solution.py:116
  102.8 1.0 copy-start.4
  103.8 34.4 %copy-start.2 = (f32[1,1024,1024]{2,1,0:T(8,128)S(1)}, f32[1,1024,1024]{2,1,0:T(8,128)}, u32[]{:S(2)}) copy-start(f32[1,1024,1024]{2,1,0:T(8,128)} %refs_16_.3) | copy-start | bytes 12582916
  113.9 10.9 %copy-start.7 = (bf16[256,256]{1,0:T(8,128)(2,1)S(1)}, bf16[256,256]{1,0:T(8,128)(2,1)}, u32[]{:S(2)}) copy-start(bf16[256,256]{1,0:T(8,128)(2,1)} %get-tuple-element.56) | copy-start | bytes 393220
  113.9 14.7 %copy-start.6 = (bf16[256,256]{1,0:T(8,128)(2,1)S(1)}, bf16[256,256]{1,0:T(8,128)(2,1)}, u32[]{:S(2)}) copy-start(bf16[256,256]{1,0:T(8,128)(2,1)} %get-tuple-element.60) | copy-start | bytes 393220
  113.9 9.2 %collective-permute-start.21 = (f32[768,512]{1,0:T(8,128)S(1)}, f32[768,512]{1,0:T(8,128)S(1)}, u32[]{:S(2)}, u32[]{:S(2)}) collective-permute-start(f32[768,512]{1,0:T(8,128)S(1)} %get-tuple-element.66), channel_id=1, source_target_pairs={{0,8},{8,0},{16,24},{24,16},{1,9},{9,1},{17,25},{25,17},{2,10},{10... | collective-permute-start | bytes 4718600 | tf_op jit(solution)/shard_map/ppermute | solution.py:313
  123.4 19.7 %collective-permute-start.22 = (f16[768,512]{1,0:T(8,128)(2,1)S(1)}, f16[768,512]{1,0:T(8,128)(2,1)S(1)}, u32[]{:S(2)}, u32[]{:S(2)}) collective-permute-start(f16[768,512]{1,0:T(8,128)(2,1)S(1)} %add_convert_fusion), channel_id=1, source_target_pairs={{0,16},{8,24},{16,0},{24,8},{1,17},{9,25},{17,1},{25,9},{2,18},{10... | collective-permute-start | bytes 2359304 | tf_op jit(solution)/shard_map/ppermute | solution.py:323
  124.7 8.8 %collective-permute-start.13 = (bf16[256,256]{1,0:T(8,128)(2,1)S(1)}, bf16[256,256]{1,0:T(8,128)(2,1)S(1)}, u32[]{:S(2)}, u32[]{:S(2)}) collective-permute-start(bf16[256,256]{1,0:T(8,128)(2,1)S(1)} %copy-done.7), channel_id=1, source_target_pairs={{0,5},{1,4},{2,7},{3,6},{4,1},{5,0},{6,3},{7,2},{8,13},{9,12},{10,... | collective-permute-start | bytes 393224 | tf_op jit(solution)/shard_map/ppermute | solution.py:116
  128.6 9.6 %collective-permute-start.17 = (bf16[256,256]{1,0:T(8,128)(2,1)S(1)}, bf16[256,256]{1,0:T(8,128)(2,1)S(1)}, u32[]{:S(2)}, u32[]{:S(2)}) collective-permute-start(bf16[256,256]{1,0:T(8,128)(2,1)S(1)} %copy-done.6), channel_id=1, source_target_pairs={{0,7},{1,6},{2,5},{3,4},{4,3},{5,2},{6,1},{7,0},{8,15},{9,14},{10,... | collective-permute-start | bytes 393224 | tf_op jit(solution)/shard_map/ppermute | solution.py:116
  142.6 2.1 %collective-permute-start.18 = (f32[256,512]{1,0:T(8,128)S(1)}, f32[256,512]{1,0:T(8,128)S(1)}, u32[]{:S(2)}, u32[]{:S(2)}) collective-permute-start(f32[256,512]{1,0:T(8,128)S(1)} %get-tuple-element.62), channel_id=1, source_target_pairs={{0,8},{8,0},{16,24},{24,16},{1,9},{9,1},{17,25},{25,17},{2,10},{10... | collective-permute-start | bytes 1572872 | tf_op jit(solution)/shard_map/ppermute | solution.py:313
  143.4 10.3 %collective-permute-start.23 = (f32[768,512]{1,0:T(8,128)S(1)}, f32[768,512]{1,0:T(8,128)S(1)}, u32[]{:S(2)}, u32[]{:S(2)}) collective-permute-start(f32[768,512]{1,0:T(8,128)S(1)} %add_multiply_fusion.mine), channel_id=1, source_target_pairs={{0,8},{8,0},{16,24},{24,16},{1,9},{9,1},{17,25},{25,17},{2,10},{10... | collective-permute-start | bytes 4718600 | tf_op jit(solution)/shard_map/ppermute | solution.py:329
  144.8 7.6 %collective-permute-start.19 = (f16[256,512]{1,0:T(8,128)(2,1)S(1)}, f16[256,512]{1,0:T(8,128)(2,1)S(1)}, u32[]{:S(2)}, u32[]{:S(2)}) collective-permute-start(f16[256,512]{1,0:T(8,128)(2,1)S(1)} %add_convert_fusion.1), channel_id=1, source_target_pairs={{0,16},{8,24},{16,0},{24,8},{1,17},{9,25},{17,1},{25,9},{2,18},{10... | collective-permute-start | bytes 786440 | tf_op jit(solution)/shard_map/ppermute | solution.py:323
  152.5 4.6 %collective-permute-start.20 = (f32[256,512]{1,0:T(8,128)S(1)}, f32[256,512]{1,0:T(8,128)S(1)}, u32[]{:S(2)}, u32[]{:S(2)}) collective-permute-start(f32[256,512]{1,0:T(8,128)S(1)} %add_multiply_fusion.1.mine), channel_id=1, source_target_pairs={{0,8},{8,0},{16,24},{24,16},{1,9},{9,1},{17,25},{25,17},{2,10},{10... | collective-permute-start | bytes 1572872 | tf_op jit(solution)/shard_map/ppermute | solution.py:329

commit v3 on v2

--- a/solution.py
+++ b/solution.py
@@ -22,7 +22,7 @@
 SPLIT_VMEM = 60 * 1024 * 1024
 
 
-ORDER = ("g2", "y0", "n0", "g1", "x00", "g3", "y1", "x01", "y2", "x03", "n1", "x02", "y3", "n2", "x10", "x11", "x12", "x13")
+ORDER = ("g2", "x00", "y0", "g1", "g3", "n0", "y1", "x01", "y2", "x03", "n1", "x02", "y3", "n2", "x10", "x12", "x11", "x13")
 WINDOW = 5
 SIZES = (6, 2)
 SENT = (6, 2)

time: 159 us -> 156 us (0.981)
  waiting for transfers between devices: 103 us -> 76.1 us
  starting transfers between devices: 28.9 us -> 52.3 us
    ppermute x18, starting transfers between devices: 18.8 us -> 47.4 us  [exchange(): moved = lax.ppermute(value, 'fsdp', pairs(n, k))]
    ppermute x18, waiting for transfers between devices: 91.7 us -> 64.6 us  [exchange(): moved = lax.ppermute(value, 'fsdp', pairs(n, k))]
    ppermute x2, starting transfers between devices: 6.66 us -> 1.94 us  [shards(): got = lax.ppermute(send, 'worker', pairs(replicas, 1))]
where the time goes in v3:
time: 156 us; the launch traced here: 155 us
  waiting for transfers between devices  76.1 us (49%)
  starting transfers between devices  52.3 us (34%)
  Pallas kernels  23.7 us (15%)
    ppermute x18, waiting for transfers between devices, exchange(): moved = lax.ppermute(value, 'fsdp', pairs(n, k))  64.6 us
    ppermute x18, starting transfers between devices, exchange(): moved = lax.ppermute(value, 'fsdp', pairs(n, k))  47.4 us
    pallas_call x2, Pallas kernels, inner_step(): pl.pallas_call(functools.partial(step_kernel, n, at, share, scale), grid_...  14.3 us
    ppermute x2, waiting for transfers between devices, shards(): got = lax.ppermute(half, 'worker', pairs(replicas, k))  7.27 us
    pallas_call x2, Pallas kernels, outer_step(): pl.pallas_call(functools.partial(outer_kernel, at, share), in_specs=[pl.B...  4.88 us
    pallas_call x1, Pallas kernels, split_columns(): pl.pallas_call(functools.partial(split_kernel, n, rows, pieces), in_specs...  4.47 us
    ppermute x2, waiting for transfers between devices, shards(): got = lax.ppermute(send, 'worker', pairs(replicas, 1))  4.19 us
  transfers between devices with their start and end apart: 24, of which 12 were waited for; matrix products, arithmetic and copies ran while one was open for 1% of the time, Pallas kernels for 14%

profile of v3, /device:TPU:9, one launch (start us, length us, event | category | flops | bytes accessed | tf_op | source)
XLA Modules:
  0.0 155.3 jit_solution(18314286734417718450)
XLA Ops:
  0.6 2.4 %collective-permute-start = (bf16[256,1024]{1,0:T(8,128)(2,1)}, bf16[256,1024]{1,0:T(8,128)(2,1)S(1)}, u32[]{:S(2)}, u32[]{:S(2)}) collective-permute-start(bf16[256,1024]{1,0:T(8,128)(2,1)} %bitcast.5), channel_id=1, source_target_pairs={{0,4},{1,5},{2,6},{3,7},{4,0},{5,1},{6,2},{7,3},{8,12},{9,13},{10,... | collective-permute-start | bytes 1572872 | tf_op jit(solution)/shard_map/ppermute | solution.py:116
  3.0 0.2 collective-permute-start.3
  3.2 1.2 collective-permute-start.14
  4.4 0.6 pad_add_fusion.info
  5.0 4.5 %split_columns.1 = (bf16[256,1024]{1,0:T(8,128)(2,1)}, bf16[256,1024]{1,0:T(8,128)(2,1)}, bf16[256,1024]{1,0:T(8,128)(2,1)}, bf16[256,1024]{1,0:T(8,128)(2,1)}, ...) custom-call(s32[3]{0:T(128)} %pad_add_fusion.info, ...), custom_call_target="tpu_custom_call" | custom-call | tf_op jit(solution)/shard_map/split_columns/pallas_call | solution.py:75
  9.5 0.1 collective-permute-start.10
  9.6 17.0 %collective-permute-done.refs_12_ = bf16[256,1024]{1,0:T(8,128)(2,1)S(1)} collective-permute-done((bf16[256,1024]{1,0:T(8,128)(2,1)}, bf16[256,1024]{1,0:T(8,128)(2,1)S(1)}, u32[]{:S(2)}, u32[]{:S(2)}) %collective-permute-start) | collective-permute-done | bytes 524320 | tf_op jit(solution)/shard_map/ppermute | solution.py:116
  26.6 1.2 collective-permute-start.1
  27.8 0.0 collective-permute-done.3.refs_10_
  27.8 0.2 collective-permute-start.4
  28.1 14.9 %collective-permute-done.10.refs_4_ = bf16[256,768]{1,0:T(8,128)(2,1)S(1)} collective-permute-done((bf16[256,768]{1,0:T(8,128)(2,1)}, bf16[256,768]{1,0:T(8,128)(2,1)S(1)}, u32[]{:S(2)}, u32[]{:S(2)}) %collective-permute-start.10) | collective-permute-done | bytes 393248 | tf_op jit(solution)/shard_map/ppermute | solution.py:116
  43.0 1.2 collective-permute-start.11
  44.2 0.0 collective-permute-done.14.refs_9_
  44.2 0.0 collective-permute-start.15
  44.2 4.2 %collective-permute-start.2 = (bf16[256,1024]{1,0:T(8,128)(2,1)}, bf16[256,1024]{1,0:T(8,128)(2,1)S(1)}, u32[]{:S(2)}, u32[]{:S(2)}) collective-permute-start(bf16[256,1024]{1,0:T(8,128)(2,1)} %get-tuple-element.41), channel_id=1, source_target_pairs={{0,2},{1,3},{2,0},{3,1},{4,6},{5,7},{6,4},{7,5},{8,10},{9,11},{10,... | collective-permute-start | bytes 1572872 | tf_op jit(solution)/shard_map/ppermute | solution.py:116
  48.4 2.1 %collective-permute-done.4.refs_13_ = bf16[256,1024]{1,0:T(8,128)(2,1)S(1)} collective-permute-done((bf16[256,1024]{1,0:T(8,128)(2,1)S(1)}, bf16[256,1024]{1,0:T(8,128)(2,1)S(1)}, u32[]{:S(2)}, u32[]{:S(2)}) %collective-permute-start.4) | collective-permute-done | bytes 524320 | tf_op jit(solution)/shard_map/ppermute | solution.py:116
  50.5 0.0 collective-permute-start.5
  50.5 8.1 %collective-permute-start.7 = (bf16[256,768]{1,0:T(8,128)(2,1)}, bf16[256,768]{1,0:T(8,128)(2,1)S(1)}, u32[]{:S(2)}, u32[]{:S(2)}) collective-permute-start(bf16[256,768]{1,0:T(8,128)(2,1)} %get-tuple-element.54), channel_id=1, source_target_pairs={{0,7},{1,6},{2,5},{3,4},{4,3},{5,2},{6,1},{7,0},{8,15},{9,14},{10,... | collective-permute-start | bytes 1179656 | tf_op jit(solution)/shard_map/ppermute | solution.py:116
  58.6 4.1 %collective-permute-done.15.refs_6_ = bf16[256,768]{1,0:T(8,128)(2,1)S(1)} collective-permute-done((bf16[256,768]{1,0:T(8,128)(2,1)}, bf16[256,768]{1,0:T(8,128)(2,1)S(1)}, u32[]{:S(2)}, u32[]{:S(2)}) %collective-permute-start.15) | collective-permute-done | bytes 393248 | tf_op jit(solution)/shard_map/ppermute | solution.py:116
  62.7 0.2 collective-permute-start.16
  63.0 3.5 %collective-permute-start.12 = (bf16[256,768]{1,0:T(8,128)(2,1)}, bf16[256,768]{1,0:T(8,128)(2,1)S(1)}, u32[]{:S(2)}, u32[]{:S(2)}) collective-permute-start(bf16[256,768]{1,0:T(8,128)(2,1)} %get-tuple-element.58), channel_id=1, source_target_pairs={{0,5},{1,4},{2,7},{3,6},{4,1},{5,0},{6,3},{7,2},{8,13},{9,12},{10,... | collective-permute-start | bytes 1179656 | tf_op jit(solution)/shard_map/ppermute | solution.py:116
  66.4 6.7 %collective-permute-done.7.refs_7_ = bf16[256,768]{1,0:T(8,128)(2,1)S(1)} collective-permute-done((bf16[256,768]{1,0:T(8,128)(2,1)}, bf16[256,768]{1,0:T(8,128)(2,1)S(1)}, u32[]{:S(2)}, u32[]{:S(2)}) %collective-permute-start.7) | collective-permute-done | bytes 393248 | tf_op jit(solution)/shard_map/ppermute | solution.py:116
  73.1 19.7 %collective-permute-start.8 = (bf16[256,256]{1,0:T(8,128)(2,1)}, bf16[256,256]{1,0:T(8,128)(2,1)S(1)}, u32[]{:S(2)}, u32[]{:S(2)}) collective-permute-start(bf16[256,256]{1,0:T(8,128)(2,1)} %get-tuple-element.55), channel_id=1, source_target_pairs={{0,4},{1,5},{2,6},{3,7},{4,0},{5,1},{6,2},{7,3},{8,12},{9,13},{10,... | collective-permute-start | bytes 393224 | tf_op jit(solution)/shard_map/ppermute | solution.py:116
  92.9 6.1 %collective-permute-done.12.refs_5_ = bf16[256,768]{1,0:T(8,128)(2,1)S(1)} collective-permute-done((bf16[256,768]{1,0:T(8,128)(2,1)}, bf16[256,768]{1,0:T(8,128)(2,1)S(1)}, u32[]{:S(2)}, u32[]{:S(2)}) %collective-permute-start.12) | collective-permute-done | bytes 393248 | tf_op jit(solution)/shard_map/ppermute | solution.py:116
  99.0 1.6 collective-permute-start.13
  100.5 2.6 %collective-permute-done.16.refs_15_ = bf16[256,1024]{1,0:T(8,128)(2,1)S(1)} collective-permute-done((bf16[256,1024]{1,0:T(8,128)(2,1)S(1)}, bf16[256,1024]{1,0:T(8,128)(2,1)S(1)}, u32[]{:S(2)}, u32[]{:S(2)}) %collective-permute-start.16) | collective-permute-done | bytes 524320 | tf_op jit(solution)/shard_map/ppermute | solution.py:116
  103.2 0.0 copy-start.4
  103.2 1.0 copy-done.4
  104.2 9.9 %inner_step.3 = (f32[768,512]{1,0:T(8,128)S(1)}, f32[768,512]{1,0:T(8,128)S(1)}) custom-call(s32[3]{0:T(128)S(1)} %copy-done.5, bf16[256,1024]{1,0:T(8,128)(2,1)S(1)} %copy-done.4, bf16[256,1024]{1,0:T(8,128)(2,1)S(1)} %collective-permute-done.1.refs_1_, bf16[256,1024]{1,0:T(8,128)(2,1)S(1)} %collective-permute-done.2.refs_2_, ...), custom_call_target="tpu_custom_call" | custom-call | tf_op jit(solution)/shard_map/inner_step/pallas_call | solution.py:198
  114.2 0.7 collective-permute-start.21
  114.9 3.0 %collective-permute-done.21 = f32[768,512]{1,0:T(8,128)S(1)} collective-permute-done((f32[768,512]{1,0:T(8,128)S(1)}, f32[768,512]{1,0:T(8,128)S(1)}, u32[]{:S(2)}, u32[]{:S(2)}) %collective-permute-start.21) | collective-permute-done | bytes 1572896 | tf_op jit(solution)/shard_map/ppermute | solution.py:313
  118.0 0.4 add_convert_fusion
  118.4 1.3 collective-permute-start.22
  119.7 3.5 %collective-permute-start.9 = (bf16[256,256]{1,0:T(8,128)(2,1)S(1)}, bf16[256,256]{1,0:T(8,128)(2,1)S(1)}, u32[]{:S(2)}, u32[]{:S(2)}) collective-permute-start(bf16[256,256]{1,0:T(8,128)(2,1)S(1)} %copy-done.7), channel_id=1, source_target_pairs={{0,5},{1,4},{2,7},{3,6},{4,1},{5,0},{6,3},{7,2},{8,13},{9,12},{10,... | collective-permute-start | bytes 393224 | tf_op jit(solution)/shard_map/ppermute | solution.py:116
  123.2 7.2 %collective-permute-done.9.refs_5_ = bf16[256,256]{1,0:T(8,128)(2,1)S(1)} collective-permute-done((bf16[256,256]{1,0:T(8,128)(2,1)S(1)}, bf16[256,256]{1,0:T(8,128)(2,1)S(1)}, u32[]{:S(2)}, u32[]{:S(2)}) %collective-permute-start.9) | collective-permute-done | bytes 131104 | tf_op jit(solution)/shard_map/ppermute | solution.py:116
  130.4 3.8 %collective-permute-done.17.refs_7_ = bf16[256,256]{1,0:T(8,128)(2,1)S(1)} collective-permute-done((bf16[256,256]{1,0:T(8,128)(2,1)S(1)}, bf16[256,256]{1,0:T(8,128)(2,1)S(1)}, u32[]{:S(2)}, u32[]{:S(2)}) %collective-permute-start.17) | collective-permute-done | bytes 131104 | tf_op jit(solution)/shard_map/ppermute | solution.py:116
  134.2 4.4 %inner_step.2 = (f32[256,512]{1,0:T(8,128)S(1)}, f32[256,512]{1,0:T(8,128)S(1)}) custom-call(s32[3]{0:T(128)S(1)} %copy-done.5, bf16[256,1024]{1,0:T(8,128)(2,1)S(1)} %copy-done.4, bf16[256,1024]{1,0:T(8,128)(2,1)S(1)} %collective-permute-done.1.refs_1_, bf16[256,1024]{1,0:T(8,128)(2,1)S(1)} %collective-permute-done.2.refs_2_, ...), custom_call_target="tpu_custom_call" | custom-call | tf_op jit(solution)/shard_map/inner_step/pallas_call | solution.py:198
  138.6 1.2 collective-permute-start.18
  139.8 0.3 add_multiply_fusion.mine
  140.1 0.1 collective-permute-start.23
  140.2 1.1 collective-permute-done.18
  141.4 0.1 add_convert_fusion.1
  141.5 0.3 collective-permute-start.19
  141.8 7.3 %collective-permute-done.19 = f16[256,512]{1,0:T(8,128)(2,1)S(1)} collective-permute-done((f16[256,512]{1,0:T(8,128)(2,1)S(1)}, f16[256,512]{1,0:T(8,128)(2,1)S(1)}, u32[]{:S(2)}, u32[]{:S(2)}) %collective-permute-start.19) | collective-permute-done | bytes 262176 | tf_op jit(solution)/shard_map/ppermute | solution.py:323
  149.1 0.1 add_multiply_fusion.1.mine
  149.2 1.3 collective-permute-start.20
  150.4 3.3 %outer_step.2 = (f32[1024,1024]{1,0:T(8,128)}, f32[256,1024]{1,0:T(8,128)}) custom-call(s32[3]{0:T(128)S(1)} %copy-done.5, f32[768,512]{1,0:T(8,128)S(1)} %add_multiply_fusion.mine, f32[768,512]{1,0:T(8,128)S(1)} %collective-permute-done.23.other, f32[256,1024]{1,0:T(8,128)S(1)} %copy-done, f32[256,1024]{1,0:T(8,128)S(1)} %copy-done.1), custom_call_target="tpu_custom_call" | custom-call | tf_op jit(solution)/shard_map/outer_step/pallas_call | solution.py:259
  153.8 1.5 outer_step.3
  (26 shorter events, 0.1 us)
Async XLA Ops:
  0.6 26.0 %collective-permute-start = (bf16[256,1024]{1,0:T(8,128)(2,1)}, bf16[256,1024]{1,0:T(8,128)(2,1)S(1)}, u32[]{:S(2)}, u32[]{:S(2)}) collective-permute-start(bf16[256,1024]{1,0:T(8,128)(2,1)} %bitcast.5), channel_id=1, source_target_pairs={{0,4},{1,5},{2,6},{3,7},{4,0},{5,1},{6,2},{7,3},{8,12},{9,13},{10,... | collective-permute-start | bytes 1572872 | tf_op jit(solution)/shard_map/ppermute | solution.py:116
  3.0 24.8 %collective-permute-start.3 = (bf16[256,1024]{1,0:T(8,128)(2,1)}, bf16[256,1024]{1,0:T(8,128)(2,1)S(1)}, u32[]{:S(2)}, u32[]{:S(2)}) collective-permute-start(bf16[256,1024]{1,0:T(8,128)(2,1)} %bitcast.6), channel_id=1, source_target_pairs={{0,2},{1,3},{2,0},{3,1},{4,6},{5,7},{6,4},{7,5},{8,10},{9,11},{10,... | collective-permute-start | bytes 1572872 | tf_op jit(solution)/shard_map/ppermute | solution.py:116
  3.2 41.1 %collective-permute-start.14 = (bf16[256,1024]{1,0:T(8,128)(2,1)}, bf16[256,1024]{1,0:T(8,128)(2,1)}, u32[]{:S(2)}, u32[]{:S(2)}) collective-permute-start(bf16[256,1024]{1,0:T(8,128)(2,1)} %bitcast.7), channel_id=1, source_target_pairs={{0,1},{1,0},{2,3},{3,2},{4,5},{5,4},{6,7},{7,6},{8,9},{9,8},{10,11... | collective-permute-start | bytes 1572872 | tf_op jit(solution)/shard_map/ppermute | solution.py:116
  5.0 98.2 %copy-start = (f32[256,1024]{1,0:T(8,128)S(1)}, f32[256,1024]{1,0:T(8,128)}, u32[]{:S(2)}) copy-start(f32[256,1024]{1,0:T(8,128)} %anchor.3) | copy-start | bytes 3145732
  5.0 98.2 %copy-start.1 = (f32[256,1024]{1,0:T(8,128)S(1)}, f32[256,1024]{1,0:T(8,128)}, u32[]{:S(2)}) copy-start(f32[256,1024]{1,0:T(8,128)} %momentum.3) | copy-start | bytes 3145732
  5.0 98.2 %copy-start.3 = (bf16[1,256,1024]{2,1,0:T(8,128)(2,1)S(1)}, bf16[1,256,1024]{2,1,0:T(8,128)(2,1)}, u32[]{:S(2)}) copy-start(bf16[1,256,1024]{2,1,0:T(8,128)(2,1)} %param.8) | copy-start | bytes 1572868
  5.0 98.2 %copy-start.5 = (s32[3]{0:T(128)S(1)}, s32[3]{0:T(128)}, u32[]{:S(2)}) copy-start(s32[3]{0:T(128)} %pad_add_fusion.info) | copy-start | bytes 40
  9.5 33.5 %collective-permute-start.10 = (bf16[256,768]{1,0:T(8,128)(2,1)}, bf16[256,768]{1,0:T(8,128)(2,1)S(1)}, u32[]{:S(2)}, u32[]{:S(2)}) collective-permute-start(bf16[256,768]{1,0:T(8,128)(2,1)} %get-tuple-element.47), channel_id=1, source_target_pairs={{0,4},{1,5},{2,6},{3,7},{4,0},{5,1},{6,2},{7,3},{8,12},{9,13},{10,... | collective-permute-start | bytes 1179656 | tf_op jit(solution)/shard_map/ppermute | solution.py:116
  26.6 17.6 %collective-permute-start.1 = (bf16[256,1024]{1,0:T(8,128)(2,1)}, bf16[256,1024]{1,0:T(8,128)(2,1)S(1)}, u32[]{:S(2)}, u32[]{:S(2)}) collective-permute-start(bf16[256,1024]{1,0:T(8,128)(2,1)} %get-tuple-element.39), channel_id=1, source_target_pairs={{0,1},{1,0},{2,3},{3,2},{4,5},{5,4},{6,7},{7,6},{8,9},{9,8},{10,11... | collective-permute-start | bytes 1572872 | tf_op jit(solution)/shard_map/ppermute | solution.py:116
  27.8 22.7 %collective-permute-start.4 = (bf16[256,1024]{1,0:T(8,128)(2,1)S(1)}, bf16[256,1024]{1,0:T(8,128)(2,1)S(1)}, u32[]{:S(2)}, u32[]{:S(2)}) collective-permute-start(bf16[256,1024]{1,0:T(8,128)(2,1)S(1)} %collective-permute-done.refs_12_), channel_id=1, source_target_pairs={{0,1},{1,0},{2,3},{3,2},{4,5},{5,4},{6,7},{7,6},{8,9},{9,8},{10,11... | collective-permute-start | bytes 1572872 | tf_op jit(solution)/shard_map/ppermute | solution.py:116
  28.1 22.5 %collective-permute-start.6 = (bf16[256,1024]{1,0:T(8,128)(2,1)S(1)}, bf16[256,1024]{1,0:T(8,128)(2,1)S(1)}, u32[]{:S(2)}, u32[]{:S(2)}) collective-permute-start(bf16[256,1024]{1,0:T(8,128)(2,1)S(1)} %collective-permute-done.refs_12_), channel_id=1, source_target_pairs={{0,2},{1,3},{2,0},{3,1},{4,6},{5,7},{6,4},{7,5},{8,10},{9,11},{10,... | collective-permute-start | bytes 1572872 | tf_op jit(solution)/shard_map/ppermute | solution.py:116
  43.0 20.0 %collective-permute-start.11 = (bf16[256,1024]{1,0:T(8,128)(2,1)S(1)}, bf16[256,1024]{1,0:T(8,128)(2,1)S(1)}, u32[]{:S(2)}, u32[]{:S(2)}) collective-permute-start(bf16[256,1024]{1,0:T(8,128)(2,1)S(1)} %collective-permute-done.3.refs_10_), channel_id=1, source_target_pairs={{0,1},{1,0},{2,3},{3,2},{4,5},{5,4},{6,7},{7,6},{8,9},{9,8},{10,11... | collective-permute-start | bytes 1572872 | tf_op jit(solution)/shard_map/ppermute | solution.py:116
  44.2 18.5 %collective-permute-start.15 = (bf16[256,768]{1,0:T(8,128)(2,1)}, bf16[256,768]{1,0:T(8,128)(2,1)S(1)}, u32[]{:S(2)}, u32[]{:S(2)}) collective-permute-start(bf16[256,768]{1,0:T(8,128)(2,1)} %get-tuple-element.60), channel_id=1, source_target_pairs={{0,6},{1,7},{2,4},{3,5},{4,2},{5,3},{6,0},{7,1},{8,14},{9,15},{10,... | collective-permute-start | bytes 1179656 | tf_op jit(solution)/shard_map/ppermute | solution.py:116
  44.2 56.3 %collective-permute-start.2 = (bf16[256,1024]{1,0:T(8,128)(2,1)}, bf16[256,1024]{1,0:T(8,128)(2,1)S(1)}, u32[]{:S(2)}, u32[]{:S(2)}) collective-permute-start(bf16[256,1024]{1,0:T(8,128)(2,1)} %get-tuple-element.41), channel_id=1, source_target_pairs={{0,2},{1,3},{2,0},{3,1},{4,6},{5,7},{6,4},{7,5},{8,10},{9,11},{10,... | collective-permute-start | bytes 1572872 | tf_op jit(solution)/shard_map/ppermute | solution.py:116
  50.5 50.0 %collective-permute-start.5 = (bf16[256,1024]{1,0:T(8,128)(2,1)}, bf16[256,1024]{1,0:T(8,128)(2,1)S(1)}, u32[]{:S(2)}, u32[]{:S(2)}) collective-permute-start(bf16[256,1024]{1,0:T(8,128)(2,1)} %get-tuple-element.44), channel_id=1, source_target_pairs={{0,3},{1,2},{2,1},{3,0},{4,7},{5,6},{6,5},{7,4},{8,11},{9,10},{10,... | collective-permute-start | bytes 1572872 | tf_op jit(solution)/shard_map/ppermute | solution.py:116
  50.5 22.6 %collective-permute-start.7 = (bf16[256,768]{1,0:T(8,128)(2,1)}, bf16[256,768]{1,0:T(8,128)(2,1)S(1)}, u32[]{:S(2)}, u32[]{:S(2)}) collective-permute-start(bf16[256,768]{1,0:T(8,128)(2,1)} %get-tuple-element.54), channel_id=1, source_target_pairs={{0,7},{1,6},{2,5},{3,4},{4,3},{5,2},{6,1},{7,0},{8,15},{9,14},{10,... | collective-permute-start | bytes 1179656 | tf_op jit(solution)/shard_map/ppermute | solution.py:116
  62.7 40.4 %collective-permute-start.16 = (bf16[256,1024]{1,0:T(8,128)(2,1)S(1)}, bf16[256,1024]{1,0:T(8,128)(2,1)S(1)}, u32[]{:S(2)}, u32[]{:S(2)}) collective-permute-start(bf16[256,1024]{1,0:T(8,128)(2,1)S(1)} %collective-permute-done.6.refs_14_), channel_id=1, source_target_pairs={{0,1},{1,0},{2,3},{3,2},{4,5},{5,4},{6,7},{7,6},{8,9},{9,8},{10,11... | collective-permute-start | bytes 1572872 | tf_op jit(solution)/shard_map/ppermute | solution.py:116
  63.0 36.0 %collective-permute-start.12 = (bf16[256,768]{1,0:T(8,128)(2,1)}, bf16[256,768]{1,0:T(8,128)(2,1)S(1)}, u32[]{:S(2)}, u32[]{:S(2)}) collective-permute-start(bf16[256,768]{1,0:T(8,128)(2,1)} %get-tuple-element.58), channel_id=1, source_target_pairs={{0,5},{1,4},{2,7},{3,6},{4,1},{5,0},{6,3},{7,2},{8,13},{9,12},{10,... | collective-permute-start | bytes 1179656 | tf_op jit(solution)/shard_map/ppermute | solution.py:116
  73.1 41.1 %collective-permute-start.8 = (bf16[256,256]{1,0:T(8,128)(2,1)}, bf16[256,256]{1,0:T(8,128)(2,1)S(1)}, u32[]{:S(2)}, u32[]{:S(2)}) collective-permute-start(bf16[256,256]{1,0:T(8,128)(2,1)} %get-tuple-element.55), channel_id=1, source_target_pairs={{0,4},{1,5},{2,6},{3,7},{4,0},{5,1},{6,2},{7,3},{8,12},{9,13},{10,... | collective-permute-start | bytes 393224 | tf_op jit(solution)/shard_map/ppermute | solution.py:116
  99.0 15.2 %collective-permute-start.13 = (bf16[256,256]{1,0:T(8,128)(2,1)}, bf16[256,256]{1,0:T(8,128)(2,1)S(1)}, u32[]{:S(2)}, u32[]{:S(2)}) collective-permute-start(bf16[256,256]{1,0:T(8,128)(2,1)} %get-tuple-element.59), channel_id=1, source_target_pairs={{0,6},{1,7},{2,4},{3,5},{4,2},{5,3},{6,0},{7,1},{8,14},{9,15},{10,... | collective-permute-start | bytes 393224 | tf_op jit(solution)/shard_map/ppermute | solution.py:116
  103.2 1.0 copy-start.4
  104.2 30.0 %copy-start.2 = (f32[1,1024,1024]{2,1,0:T(8,128)S(1)}, f32[1,1024,1024]{2,1,0:T(8,128)}, u32[]{:S(2)}) copy-start(f32[1,1024,1024]{2,1,0:T(8,128)} %refs_16_.3) | copy-start | bytes 12582916
  114.2 5.4 %copy-start.7 = (bf16[256,256]{1,0:T(8,128)(2,1)S(1)}, bf16[256,256]{1,0:T(8,128)(2,1)}, u32[]{:S(2)}) copy-start(bf16[256,256]{1,0:T(8,128)(2,1)} %get-tuple-element.56) | copy-start | bytes 393220
  114.2 9.0 %copy-start.6 = (bf16[256,256]{1,0:T(8,128)(2,1)S(1)}, bf16[256,256]{1,0:T(8,128)(2,1)}, u32[]{:S(2)}) copy-start(bf16[256,256]{1,0:T(8,128)(2,1)} %get-tuple-element.62) | copy-start | bytes 393220
  114.2 3.8 %collective-permute-start.21 = (f32[768,512]{1,0:T(8,128)S(1)}, f32[768,512]{1,0:T(8,128)S(1)}, u32[]{:S(2)}, u32[]{:S(2)}) collective-permute-start(f32[768,512]{1,0:T(8,128)S(1)} %get-tuple-element.68), channel_id=1, source_target_pairs={{0,8},{8,0},{16,24},{24,16},{1,9},{9,1},{17,25},{25,17},{2,10},{10... | collective-permute-start | bytes 4718600 | tf_op jit(solution)/shard_map/ppermute | solution.py:313
  118.4 21.4 %collective-permute-start.22 = (f16[768,512]{1,0:T(8,128)(2,1)S(1)}, f16[768,512]{1,0:T(8,128)(2,1)S(1)}, u32[]{:S(2)}, u32[]{:S(2)}) collective-permute-start(f16[768,512]{1,0:T(8,128)(2,1)S(1)} %add_convert_fusion), channel_id=1, source_target_pairs={{0,16},{8,24},{16,0},{24,8},{1,17},{9,25},{17,1},{25,9},{2,18},{10... | collective-permute-start | bytes 2359304 | tf_op jit(solution)/shard_map/ppermute | solution.py:323
  119.7 10.7 %collective-permute-start.9 = (bf16[256,256]{1,0:T(8,128)(2,1)S(1)}, bf16[256,256]{1,0:T(8,128)(2,1)S(1)}, u32[]{:S(2)}, u32[]{:S(2)}) collective-permute-start(bf16[256,256]{1,0:T(8,128)(2,1)S(1)} %copy-done.7), channel_id=1, source_target_pairs={{0,5},{1,4},{2,7},{3,6},{4,1},{5,0},{6,3},{7,2},{8,13},{9,12},{10,... | collective-permute-start | bytes 393224 | tf_op jit(solution)/shard_map/ppermute | solution.py:116
  123.2 11.0 %collective-permute-start.17 = (bf16[256,256]{1,0:T(8,128)(2,1)S(1)}, bf16[256,256]{1,0:T(8,128)(2,1)S(1)}, u32[]{:S(2)}, u32[]{:S(2)}) collective-permute-start(bf16[256,256]{1,0:T(8,128)(2,1)S(1)} %copy-done.6), channel_id=1, source_target_pairs={{0,7},{1,6},{2,5},{3,4},{4,3},{5,2},{6,1},{7,0},{8,15},{9,14},{10,... | collective-permute-start | bytes 393224 | tf_op jit(solution)/shard_map/ppermute | solution.py:116
  138.6 2.8 %collective-permute-start.18 = (f32[256,512]{1,0:T(8,128)S(1)}, f32[256,512]{1,0:T(8,128)S(1)}, u32[]{:S(2)}, u32[]{:S(2)}) collective-permute-start(f32[256,512]{1,0:T(8,128)S(1)} %get-tuple-element.64), channel_id=1, source_target_pairs={{0,8},{8,0},{16,24},{24,16},{1,9},{9,1},{17,25},{25,17},{2,10},{10... | collective-permute-start | bytes 1572872 | tf_op jit(solution)/shard_map/ppermute | solution.py:313
  140.1 10.3 %collective-permute-start.23 = (f32[768,512]{1,0:T(8,128)S(1)}, f32[768,512]{1,0:T(8,128)S(1)}, u32[]{:S(2)}, u32[]{:S(2)}) collective-permute-start(f32[768,512]{1,0:T(8,128)S(1)} %add_multiply_fusion.mine), channel_id=1, source_target_pairs={{0,8},{8,0},{16,24},{24,16},{1,9},{9,1},{17,25},{25,17},{2,10},{10... | collective-permute-start | bytes 4718600 | tf_op jit(solution)/shard_map/ppermute | solution.py:329
  141.5 7.6 %collective-permute-start.19 = (f16[256,512]{1,0:T(8,128)(2,1)S(1)}, f16[256,512]{1,0:T(8,128)(2,1)S(1)}, u32[]{:S(2)}, u32[]{:S(2)}) collective-permute-start(f16[256,512]{1,0:T(8,128)(2,1)S(1)} %add_convert_fusion.1), channel_id=1, source_target_pairs={{0,16},{8,24},{16,0},{24,8},{1,17},{9,25},{17,1},{25,9},{2,18},{10... | collective-permute-start | bytes 786440 | tf_op jit(solution)/shard_map/ppermute | solution.py:323
  149.2 4.6 %collective-permute-start.20 = (f32[256,512]{1,0:T(8,128)S(1)}, f32[256,512]{1,0:T(8,128)S(1)}, u32[]{:S(2)}, u32[]{:S(2)}) collective-permute-start(f32[256,512]{1,0:T(8,128)S(1)} %add_multiply_fusion.1.mine), channel_id=1, source_target_pairs={{0,8},{8,0},{16,24},{24,16},{1,9},{9,1},{17,25},{25,17},{2,10},{10... | collective-permute-start | bytes 1572872 | tf_op jit(solution)/shard_map/ppermute | solution.py:329

commit v4 on v3

--- a/solution.py
+++ b/solution.py
@@ -22,13 +22,13 @@
 SPLIT_VMEM = 60 * 1024 * 1024
 
 
-ORDER = ("g2", "x00", "y0", "g1", "g3", "n0", "y1", "x01", "y2", "x03", "n1", "x02", "y3", "n2", "x10", "x12", "x11", "x13")
+ORDER = ("g2", "x00", "g1", "y0", "g3", "n0", "y1", "x01", "y2", "x03", "n1", "x02", "y3", "n2", "x10", "x12", "x11", "x13")
 WINDOW = 5
 SIZES = (6, 2)
 SENT = (6, 2)
 STEP_PINS = (("x10", "x11"),)
 CORE_PINS = ((),)
-CHIP_PINS = (("x12",),)
+CHIP_PINS = (("x12", "x13"),)
 BLOCK = 256
 
 

time: 156 us -> 155 us (level)
  no operation moved by 1% of the time
where the time goes in v4:
time: 155 us
  waiting for transfers between devices  76.2 us (49%)
  starting transfers between devices  52.1 us (34%)
  Pallas kernels  23.6 us (15%)
    ppermute x18, waiting for transfers between devices, exchange(): moved = lax.ppermute(value, 'fsdp', pairs(n, k))  64.8 us
    ppermute x18, starting transfers between devices, exchange(): moved = lax.ppermute(value, 'fsdp', pairs(n, k))  47.2 us
    pallas_call x2, Pallas kernels, inner_step(): pl.pallas_call(functools.partial(step_kernel, n, at, share, scale), grid_...  14.3 us
    ppermute x2, waiting for transfers between devices, shards(): got = lax.ppermute(half, 'worker', pairs(replicas, k))  7.27 us
    pallas_call x2, Pallas kernels, outer_step(): pl.pallas_call(functools.partial(outer_kernel, at, share), in_specs=[pl.B...  4.88 us
    pallas_call x1, Pallas kernels, split_columns(): pl.pallas_call(functools.partial(split_kernel, n, rows, pieces), in_specs...  4.47 us
    ppermute x2, waiting for transfers between devices, shards(): got = lax.ppermute(send, 'worker', pairs(replicas, 1))  4.19 us
  transfers between devices with their start and end apart: 24, of which 12 were waited for; matrix products, arithmetic and copies ran while one was open for 1% of the time, Pallas kernels for 14%

profile of v4, /device:TPU:9, one launch (start us, length us, event | category | flops | bytes accessed | tf_op | source)
XLA Modules:
  0.0 155.2 jit_solution(708480321595137224)
XLA Ops:
  0.6 2.4 %collective-permute-start = (bf16[256,1024]{1,0:T(8,128)(2,1)}, bf16[256,1024]{1,0:T(8,128)(2,1)S(1)}, u32[]{:S(2)}, u32[]{:S(2)}) collective-permute-start(bf16[256,1024]{1,0:T(8,128)(2,1)} %bitcast.5), channel_id=1, source_target_pairs={{0,4},{1,5},{2,6},{3,7},{4,0},{5,1},{6,2},{7,3},{8,12},{9,13},{10,... | collective-permute-start | bytes 1572872 | tf_op jit(solution)/shard_map/ppermute | solution.py:116
  3.0 1.2 collective-permute-start.3
  4.2 0.2 collective-permute-start.10
  4.4 0.6 pad_add_fusion.info
  5.0 4.5 %split_columns.1 = (bf16[256,1024]{1,0:T(8,128)(2,1)}, bf16[256,1024]{1,0:T(8,128)(2,1)}, bf16[256,1024]{1,0:T(8,128)(2,1)}, bf16[256,1024]{1,0:T(8,128)(2,1)}, ...) custom-call(s32[3]{0:T(128)} %pad_add_fusion.info, ...), custom_call_target="tpu_custom_call" | custom-call | tf_op jit(solution)/shard_map/split_columns/pallas_call | solution.py:75
  9.5 0.1 collective-permute-start.11
  9.6 17.1 %collective-permute-done.refs_12_ = bf16[256,1024]{1,0:T(8,128)(2,1)S(1)} collective-permute-done((bf16[256,1024]{1,0:T(8,128)(2,1)}, bf16[256,1024]{1,0:T(8,128)(2,1)S(1)}, u32[]{:S(2)}, u32[]{:S(2)}) %collective-permute-start) | collective-permute-done | bytes 524320 | tf_op jit(solution)/shard_map/ppermute | solution.py:116
  26.7 1.1 collective-permute-start.1
  27.8 0.3 collective-permute-start.4
  28.2 0.0 collective-permute-start.6
  28.2 14.9 %collective-permute-done.11.refs_4_ = bf16[256,768]{1,0:T(8,128)(2,1)S(1)} collective-permute-done((bf16[256,768]{1,0:T(8,128)(2,1)}, bf16[256,768]{1,0:T(8,128)(2,1)S(1)}, u32[]{:S(2)}, u32[]{:S(2)}) %collective-permute-start.11) | collective-permute-done | bytes 393248 | tf_op jit(solution)/shard_map/ppermute | solution.py:116
  43.0 0.0 collective-permute-done.10.refs_10_
  43.0 1.2 collective-permute-start.12
  44.2 0.0 collective-permute-start.15
  44.2 0.0 collective-permute-done.1.refs_1_
  44.2 4.2 %collective-permute-start.2 = (bf16[256,1024]{1,0:T(8,128)(2,1)}, bf16[256,1024]{1,0:T(8,128)(2,1)S(1)}, u32[]{:S(2)}, u32[]{:S(2)}) collective-permute-start(bf16[256,1024]{1,0:T(8,128)(2,1)} %get-tuple-element.41), channel_id=1, source_target_pairs={{0,2},{1,3},{2,0},{3,1},{4,6},{5,7},{6,4},{7,5},{8,10},{9,11},{10,... | collective-permute-start | bytes 1572872 | tf_op jit(solution)/shard_map/ppermute | solution.py:116
  48.4 2.2 %collective-permute-done.4.refs_13_ = bf16[256,1024]{1,0:T(8,128)(2,1)S(1)} collective-permute-done((bf16[256,1024]{1,0:T(8,128)(2,1)S(1)}, bf16[256,1024]{1,0:T(8,128)(2,1)S(1)}, u32[]{:S(2)}, u32[]{:S(2)}) %collective-permute-start.4) | collective-permute-done | bytes 524320 | tf_op jit(solution)/shard_map/ppermute | solution.py:116
  50.6 7.9 %collective-permute-start.7 = (bf16[256,768]{1,0:T(8,128)(2,1)}, bf16[256,768]{1,0:T(8,128)(2,1)S(1)}, u32[]{:S(2)}, u32[]{:S(2)}) collective-permute-start(bf16[256,768]{1,0:T(8,128)(2,1)} %get-tuple-element.54), channel_id=1, source_target_pairs={{0,7},{1,6},{2,5},{3,4},{4,3},{5,2},{6,1},{7,0},{8,15},{9,14},{10,... | collective-permute-start | bytes 1179656 | tf_op jit(solution)/shard_map/ppermute | solution.py:116
  58.6 4.2 %collective-permute-done.15.refs_6_ = bf16[256,768]{1,0:T(8,128)(2,1)S(1)} collective-permute-done((bf16[256,768]{1,0:T(8,128)(2,1)}, bf16[256,768]{1,0:T(8,128)(2,1)S(1)}, u32[]{:S(2)}, u32[]{:S(2)}) %collective-permute-start.15) | collective-permute-done | bytes 393248 | tf_op jit(solution)/shard_map/ppermute | solution.py:116
  62.7 0.3 collective-permute-start.16
  63.0 3.4 %collective-permute-start.13 = (bf16[256,768]{1,0:T(8,128)(2,1)}, bf16[256,768]{1,0:T(8,128)(2,1)S(1)}, u32[]{:S(2)}, u32[]{:S(2)}) collective-permute-start(bf16[256,768]{1,0:T(8,128)(2,1)} %get-tuple-element.58), channel_id=1, source_target_pairs={{0,5},{1,4},{2,7},{3,6},{4,1},{5,0},{6,3},{7,2},{8,13},{9,12},{10,... | collective-permute-start | bytes 1179656 | tf_op jit(solution)/shard_map/ppermute | solution.py:116
  66.4 6.7 %collective-permute-done.7.refs_7_ = bf16[256,768]{1,0:T(8,128)(2,1)S(1)} collective-permute-done((bf16[256,768]{1,0:T(8,128)(2,1)}, bf16[256,768]{1,0:T(8,128)(2,1)S(1)}, u32[]{:S(2)}, u32[]{:S(2)}) %collective-permute-start.7) | collective-permute-done | bytes 393248 | tf_op jit(solution)/shard_map/ppermute | solution.py:116
  73.2 19.8 %collective-permute-start.8 = (bf16[256,256]{1,0:T(8,128)(2,1)}, bf16[256,256]{1,0:T(8,128)(2,1)S(1)}, u32[]{:S(2)}, u32[]{:S(2)}) collective-permute-start(bf16[256,256]{1,0:T(8,128)(2,1)} %get-tuple-element.55), channel_id=1, source_target_pairs={{0,4},{1,5},{2,6},{3,7},{4,0},{5,1},{6,2},{7,3},{8,12},{9,13},{10,... | collective-permute-start | bytes 393224 | tf_op jit(solution)/shard_map/ppermute | solution.py:116
  92.9 6.2 %collective-permute-done.13.refs_5_ = bf16[256,768]{1,0:T(8,128)(2,1)S(1)} collective-permute-done((bf16[256,768]{1,0:T(8,128)(2,1)}, bf16[256,768]{1,0:T(8,128)(2,1)S(1)}, u32[]{:S(2)}, u32[]{:S(2)}) %collective-permute-start.13) | collective-permute-done | bytes 393248 | tf_op jit(solution)/shard_map/ppermute | solution.py:116
  99.1 1.5 collective-permute-start.14
  100.6 2.6 %collective-permute-done.16.refs_15_ = bf16[256,1024]{1,0:T(8,128)(2,1)S(1)} collective-permute-done((bf16[256,1024]{1,0:T(8,128)(2,1)S(1)}, bf16[256,1024]{1,0:T(8,128)(2,1)S(1)}, u32[]{:S(2)}, u32[]{:S(2)}) %collective-permute-start.16) | collective-permute-done | bytes 524320 | tf_op jit(solution)/shard_map/ppermute | solution.py:116
  103.2 0.0 copy-start.4
  103.3 1.0 copy-done.4
  104.3 9.9 %inner_step.3 = (f32[768,512]{1,0:T(8,128)S(1)}, f32[768,512]{1,0:T(8,128)S(1)}) custom-call(s32[3]{0:T(128)S(1)} %copy-done.5, bf16[256,1024]{1,0:T(8,128)(2,1)S(1)} %copy-done.4, bf16[256,1024]{1,0:T(8,128)(2,1)S(1)} %collective-permute-done.1.refs_1_, bf16[256,1024]{1,0:T(8,128)(2,1)S(1)} %collective-permute-done.2.refs_2_, ...), custom_call_target="tpu_custom_call" | custom-call | tf_op jit(solution)/shard_map/inner_step/pallas_call | solution.py:198
  114.2 0.7 collective-permute-start.21
  114.9 3.0 %collective-permute-done.21 = f32[768,512]{1,0:T(8,128)S(1)} collective-permute-done((f32[768,512]{1,0:T(8,128)S(1)}, f32[768,512]{1,0:T(8,128)S(1)}, u32[]{:S(2)}, u32[]{:S(2)}) %collective-permute-start.21) | collective-permute-done | bytes 1572896 | tf_op jit(solution)/shard_map/ppermute | solution.py:313
  118.0 0.4 add_convert_fusion
  118.4 1.3 collective-permute-start.22
  119.6 3.5 %collective-permute-start.9 = (bf16[256,256]{1,0:T(8,128)(2,1)S(1)}, bf16[256,256]{1,0:T(8,128)(2,1)S(1)}, u32[]{:S(2)}, u32[]{:S(2)}) collective-permute-start(bf16[256,256]{1,0:T(8,128)(2,1)S(1)} %copy-done.7), channel_id=1, source_target_pairs={{0,5},{1,4},{2,7},{3,6},{4,1},{5,0},{6,3},{7,2},{8,13},{9,12},{10,... | collective-permute-start | bytes 393224 | tf_op jit(solution)/shard_map/ppermute | solution.py:116
  123.1 7.2 %collective-permute-done.9.refs_5_ = bf16[256,256]{1,0:T(8,128)(2,1)S(1)} collective-permute-done((bf16[256,256]{1,0:T(8,128)(2,1)S(1)}, bf16[256,256]{1,0:T(8,128)(2,1)S(1)}, u32[]{:S(2)}, u32[]{:S(2)}) %collective-permute-start.9) | collective-permute-done | bytes 131104 | tf_op jit(solution)/shard_map/ppermute | solution.py:116
  130.4 3.7 %collective-permute-done.17.refs_7_ = bf16[256,256]{1,0:T(8,128)(2,1)S(1)} collective-permute-done((bf16[256,256]{1,0:T(8,128)(2,1)S(1)}, bf16[256,256]{1,0:T(8,128)(2,1)S(1)}, u32[]{:S(2)}, u32[]{:S(2)}) %collective-permute-start.17) | collective-permute-done | bytes 131104 | tf_op jit(solution)/shard_map/ppermute | solution.py:116
  134.1 4.4 %inner_step.2 = (f32[256,512]{1,0:T(8,128)S(1)}, f32[256,512]{1,0:T(8,128)S(1)}) custom-call(s32[3]{0:T(128)S(1)} %copy-done.5, bf16[256,1024]{1,0:T(8,128)(2,1)S(1)} %copy-done.4, bf16[256,1024]{1,0:T(8,128)(2,1)S(1)} %collective-permute-done.1.refs_1_, bf16[256,1024]{1,0:T(8,128)(2,1)S(1)} %collective-permute-done.2.refs_2_, ...), custom_call_target="tpu_custom_call" | custom-call | tf_op jit(solution)/shard_map/inner_step/pallas_call | solution.py:198
  138.4 1.3 collective-permute-start.18
  139.7 0.3 add_multiply_fusion.mine
  140.0 0.1 collective-permute-start.23
  140.1 1.1 collective-permute-done.18
  141.2 0.1 add_convert_fusion.1
  141.4 0.3 collective-permute-start.19
  141.7 7.3 %collective-permute-done.19 = f16[256,512]{1,0:T(8,128)(2,1)S(1)} collective-permute-done((f16[256,512]{1,0:T(8,128)(2,1)S(1)}, f16[256,512]{1,0:T(8,128)(2,1)S(1)}, u32[]{:S(2)}, u32[]{:S(2)}) %collective-permute-start.19) | collective-permute-done | bytes 262176 | tf_op jit(solution)/shard_map/ppermute | solution.py:323
  148.9 0.1 add_multiply_fusion.1.mine
  149.0 1.3 collective-permute-start.20
  150.3 3.3 %outer_step.2 = (f32[1024,1024]{1,0:T(8,128)}, f32[256,1024]{1,0:T(8,128)}) custom-call(s32[3]{0:T(128)S(1)} %copy-done.5, f32[768,512]{1,0:T(8,128)S(1)} %add_multiply_fusion.mine, f32[768,512]{1,0:T(8,128)S(1)} %collective-permute-done.23.other, f32[256,1024]{1,0:T(8,128)S(1)} %copy-done, f32[256,1024]{1,0:T(8,128)S(1)} %copy-done.1), custom_call_target="tpu_custom_call" | custom-call | tf_op jit(solution)/shard_map/outer_step/pallas_call | solution.py:259
  153.7 1.5 outer_step.3
  (26 shorter events, 0.1 us)
Async XLA Ops:
  0.6 26.1 %collective-permute-start = (bf16[256,1024]{1,0:T(8,128)(2,1)}, bf16[256,1024]{1,0:T(8,128)(2,1)S(1)}, u32[]{:S(2)}, u32[]{:S(2)}) collective-permute-start(bf16[256,1024]{1,0:T(8,128)(2,1)} %bitcast.5), channel_id=1, source_target_pairs={{0,4},{1,5},{2,6},{3,7},{4,0},{5,1},{6,2},{7,3},{8,12},{9,13},{10,... | collective-permute-start | bytes 1572872 | tf_op jit(solution)/shard_map/ppermute | solution.py:116
  3.0 24.8 %collective-permute-start.3 = (bf16[256,1024]{1,0:T(8,128)(2,1)}, bf16[256,1024]{1,0:T(8,128)(2,1)S(1)}, u32[]{:S(2)}, u32[]{:S(2)}) collective-permute-start(bf16[256,1024]{1,0:T(8,128)(2,1)} %bitcast.6), channel_id=1, source_target_pairs={{0,1},{1,0},{2,3},{3,2},{4,5},{5,4},{6,7},{7,6},{8,9},{9,8},{10,11... | collective-permute-start | bytes 1572872 | tf_op jit(solution)/shard_map/ppermute | solution.py:116
  4.2 38.8 %collective-permute-start.10 = (bf16[256,1024]{1,0:T(8,128)(2,1)}, bf16[256,1024]{1,0:T(8,128)(2,1)}, u32[]{:S(2)}, u32[]{:S(2)}) collective-permute-start(bf16[256,1024]{1,0:T(8,128)(2,1)} %bitcast.7), channel_id=1, source_target_pairs={{0,2},{1,3},{2,0},{3,1},{4,6},{5,7},{6,4},{7,5},{8,10},{9,11},{10,... | collective-permute-start | bytes 1572872 | tf_op jit(solution)/shard_map/ppermute | solution.py:116
  5.0 98.2 %copy-start = (f32[256,1024]{1,0:T(8,128)S(1)}, f32[256,1024]{1,0:T(8,128)}, u32[]{:S(2)}) copy-start(f32[256,1024]{1,0:T(8,128)} %anchor.3) | copy-start | bytes 3145732
  5.0 98.2 %copy-start.1 = (f32[256,1024]{1,0:T(8,128)S(1)}, f32[256,1024]{1,0:T(8,128)}, u32[]{:S(2)}) copy-start(f32[256,1024]{1,0:T(8,128)} %momentum.3) | copy-start | bytes 3145732
  5.0 98.2 %copy-start.3 = (bf16[1,256,1024]{2,1,0:T(8,128)(2,1)S(1)}, bf16[1,256,1024]{2,1,0:T(8,128)(2,1)}, u32[]{:S(2)}) copy-start(bf16[1,256,1024]{2,1,0:T(8,128)(2,1)} %param.8) | copy-start | bytes 1572868
  5.0 98.2 %copy-start.5 = (s32[3]{0:T(128)S(1)}, s32[3]{0:T(128)}, u32[]{:S(2)}) copy-start(s32[3]{0:T(128)} %pad_add_fusion.info) | copy-start | bytes 40
  9.5 33.6 %collective-permute-start.11 = (bf16[256,768]{1,0:T(8,128)(2,1)}, bf16[256,768]{1,0:T(8,128)(2,1)S(1)}, u32[]{:S(2)}, u32[]{:S(2)}) collective-permute-start(bf16[256,768]{1,0:T(8,128)(2,1)} %get-tuple-element.47), channel_id=1, source_target_pairs={{0,4},{1,5},{2,6},{3,7},{4,0},{5,1},{6,2},{7,3},{8,12},{9,13},{10,... | collective-permute-start | bytes 1179656 | tf_op jit(solution)/shard_map/ppermute | solution.py:116
  26.7 17.6 %collective-permute-start.1 = (bf16[256,1024]{1,0:T(8,128)(2,1)}, bf16[256,1024]{1,0:T(8,128)(2,1)S(1)}, u32[]{:S(2)}, u32[]{:S(2)}) collective-permute-start(bf16[256,1024]{1,0:T(8,128)(2,1)} %get-tuple-element.39), channel_id=1, source_target_pairs={{0,1},{1,0},{2,3},{3,2},{4,5},{5,4},{6,7},{7,6},{8,9},{9,8},{10,11... | collective-permute-start | bytes 1572872 | tf_op jit(solution)/shard_map/ppermute | solution.py:116
  27.8 22.8 %collective-permute-start.4 = (bf16[256,1024]{1,0:T(8,128)(2,1)S(1)}, bf16[256,1024]{1,0:T(8,128)(2,1)S(1)}, u32[]{:S(2)}, u32[]{:S(2)}) collective-permute-start(bf16[256,1024]{1,0:T(8,128)(2,1)S(1)} %collective-permute-done.refs_12_), channel_id=1, source_target_pairs={{0,1},{1,0},{2,3},{3,2},{4,5},{5,4},{6,7},{7,6},{8,9},{9,8},{10,11... | collective-permute-start | bytes 1572872 | tf_op jit(solution)/shard_map/ppermute | solution.py:116
  28.2 22.5 %collective-permute-start.6 = (bf16[256,1024]{1,0:T(8,128)(2,1)S(1)}, bf16[256,1024]{1,0:T(8,128)(2,1)S(1)}, u32[]{:S(2)}, u32[]{:S(2)}) collective-permute-start(bf16[256,1024]{1,0:T(8,128)(2,1)S(1)} %collective-permute-done.refs_12_), channel_id=1, source_target_pairs={{0,2},{1,3},{2,0},{3,1},{4,6},{5,7},{6,4},{7,5},{8,10},{9,11},{10,... | collective-permute-start | bytes 1572872 | tf_op jit(solution)/shard_map/ppermute | solution.py:116
  43.0 20.0 %collective-permute-start.12 = (bf16[256,1024]{1,0:T(8,128)(2,1)}, bf16[256,1024]{1,0:T(8,128)(2,1)S(1)}, u32[]{:S(2)}, u32[]{:S(2)}) collective-permute-start(bf16[256,1024]{1,0:T(8,128)(2,1)} %collective-permute-done.10.refs_10_), channel_id=1, source_target_pairs={{0,1},{1,0},{2,3},{3,2},{4,5},{5,4},{6,7},{7,6},{8,9},{9,8},{10,11... | collective-permute-start | bytes 1572872 | tf_op jit(solution)/shard_map/ppermute | solution.py:116
  44.2 18.5 %collective-permute-start.15 = (bf16[256,768]{1,0:T(8,128)(2,1)}, bf16[256,768]{1,0:T(8,128)(2,1)S(1)}, u32[]{:S(2)}, u32[]{:S(2)}) collective-permute-start(bf16[256,768]{1,0:T(8,128)(2,1)} %get-tuple-element.60), channel_id=1, source_target_pairs={{0,6},{1,7},{2,4},{3,5},{4,2},{5,3},{6,0},{7,1},{8,14},{9,15},{10,... | collective-permute-start | bytes 1179656 | tf_op jit(solution)/shard_map/ppermute | solution.py:116
  44.2 56.3 %collective-permute-start.2 = (bf16[256,1024]{1,0:T(8,128)(2,1)}, bf16[256,1024]{1,0:T(8,128)(2,1)S(1)}, u32[]{:S(2)}, u32[]{:S(2)}) collective-permute-start(bf16[256,1024]{1,0:T(8,128)(2,1)} %get-tuple-element.41), channel_id=1, source_target_pairs={{0,2},{1,3},{2,0},{3,1},{4,6},{5,7},{6,4},{7,5},{8,10},{9,11},{10,... | collective-permute-start | bytes 1572872 | tf_op jit(solution)/shard_map/ppermute | solution.py:116
  50.6 50.0 %collective-permute-start.5 = (bf16[256,1024]{1,0:T(8,128)(2,1)}, bf16[256,1024]{1,0:T(8,128)(2,1)S(1)}, u32[]{:S(2)}, u32[]{:S(2)}) collective-permute-start(bf16[256,1024]{1,0:T(8,128)(2,1)} %get-tuple-element.44), channel_id=1, source_target_pairs={{0,3},{1,2},{2,1},{3,0},{4,7},{5,6},{6,5},{7,4},{8,11},{9,10},{10,... | collective-permute-start | bytes 1572872 | tf_op jit(solution)/shard_map/ppermute | solution.py:116
  50.6 22.5 %collective-permute-start.7 = (bf16[256,768]{1,0:T(8,128)(2,1)}, bf16[256,768]{1,0:T(8,128)(2,1)S(1)}, u32[]{:S(2)}, u32[]{:S(2)}) collective-permute-start(bf16[256,768]{1,0:T(8,128)(2,1)} %get-tuple-element.54), channel_id=1, source_target_pairs={{0,7},{1,6},{2,5},{3,4},{4,3},{5,2},{6,1},{7,0},{8,15},{9,14},{10,... | collective-permute-start | bytes 1179656 | tf_op jit(solution)/shard_map/ppermute | solution.py:116
  62.7 40.5 %collective-permute-start.16 = (bf16[256,1024]{1,0:T(8,128)(2,1)S(1)}, bf16[256,1024]{1,0:T(8,128)(2,1)S(1)}, u32[]{:S(2)}, u32[]{:S(2)}) collective-permute-start(bf16[256,1024]{1,0:T(8,128)(2,1)S(1)} %collective-permute-done.6.refs_14_), channel_id=1, source_target_pairs={{0,1},{1,0},{2,3},{3,2},{4,5},{5,4},{6,7},{7,6},{8,9},{9,8},{10,11... | collective-permute-start | bytes 1572872 | tf_op jit(solution)/shard_map/ppermute | solution.py:116
  63.0 36.1 %collective-permute-start.13 = (bf16[256,768]{1,0:T(8,128)(2,1)}, bf16[256,768]{1,0:T(8,128)(2,1)S(1)}, u32[]{:S(2)}, u32[]{:S(2)}) collective-permute-start(bf16[256,768]{1,0:T(8,128)(2,1)} %get-tuple-element.58), channel_id=1, source_target_pairs={{0,5},{1,4},{2,7},{3,6},{4,1},{5,0},{6,3},{7,2},{8,13},{9,12},{10,... | collective-permute-start | bytes 1179656 | tf_op jit(solution)/shard_map/ppermute | solution.py:116
  73.2 41.0 %collective-permute-start.8 = (bf16[256,256]{1,0:T(8,128)(2,1)}, bf16[256,256]{1,0:T(8,128)(2,1)S(1)}, u32[]{:S(2)}, u32[]{:S(2)}) collective-permute-start(bf16[256,256]{1,0:T(8,128)(2,1)} %get-tuple-element.55), channel_id=1, source_target_pairs={{0,4},{1,5},{2,6},{3,7},{4,0},{5,1},{6,2},{7,3},{8,12},{9,13},{10,... | collective-permute-start | bytes 393224 | tf_op jit(solution)/shard_map/ppermute | solution.py:116
  99.1 15.1 %collective-permute-start.14 = (bf16[256,256]{1,0:T(8,128)(2,1)}, bf16[256,256]{1,0:T(8,128)(2,1)S(1)}, u32[]{:S(2)}, u32[]{:S(2)}) collective-permute-start(bf16[256,256]{1,0:T(8,128)(2,1)} %get-tuple-element.59), channel_id=1, source_target_pairs={{0,6},{1,7},{2,4},{3,5},{4,2},{5,3},{6,0},{7,1},{8,14},{9,15},{10,... | collective-permute-start | bytes 393224 | tf_op jit(solution)/shard_map/ppermute | solution.py:116
  103.2 1.0 copy-start.4
  104.3 29.8 %copy-start.2 = (f32[1,1024,1024]{2,1,0:T(8,128)S(1)}, f32[1,1024,1024]{2,1,0:T(8,128)}, u32[]{:S(2)}) copy-start(f32[1,1024,1024]{2,1,0:T(8,128)} %refs_16_.3) | copy-start | bytes 12582916
  114.2 5.4 %copy-start.7 = (bf16[256,256]{1,0:T(8,128)(2,1)S(1)}, bf16[256,256]{1,0:T(8,128)(2,1)}, u32[]{:S(2)}) copy-start(bf16[256,256]{1,0:T(8,128)(2,1)} %get-tuple-element.56) | copy-start | bytes 393220
  114.2 8.9 %copy-start.6 = (bf16[256,256]{1,0:T(8,128)(2,1)S(1)}, bf16[256,256]{1,0:T(8,128)(2,1)}, u32[]{:S(2)}) copy-start(bf16[256,256]{1,0:T(8,128)(2,1)} %get-tuple-element.62) | copy-start | bytes 393220
  114.2 3.8 %collective-permute-start.21 = (f32[768,512]{1,0:T(8,128)S(1)}, f32[768,512]{1,0:T(8,128)S(1)}, u32[]{:S(2)}, u32[]{:S(2)}) collective-permute-start(f32[768,512]{1,0:T(8,128)S(1)} %get-tuple-element.68), channel_id=1, source_target_pairs={{0,8},{8,0},{16,24},{24,16},{1,9},{9,1},{17,25},{25,17},{2,10},{10... | collective-permute-start | bytes 4718600 | tf_op jit(solution)/shard_map/ppermute | solution.py:313
  118.4 21.3 %collective-permute-start.22 = (f16[768,512]{1,0:T(8,128)(2,1)S(1)}, f16[768,512]{1,0:T(8,128)(2,1)S(1)}, u32[]{:S(2)}, u32[]{:S(2)}) collective-permute-start(f16[768,512]{1,0:T(8,128)(2,1)S(1)} %add_convert_fusion), channel_id=1, source_target_pairs={{0,16},{8,24},{16,0},{24,8},{1,17},{9,25},{17,1},{25,9},{2,18},{10... | collective-permute-start | bytes 2359304 | tf_op jit(solution)/shard_map/ppermute | solution.py:323
  119.6 10.7 %collective-permute-start.9 = (bf16[256,256]{1,0:T(8,128)(2,1)S(1)}, bf16[256,256]{1,0:T(8,128)(2,1)S(1)}, u32[]{:S(2)}, u32[]{:S(2)}) collective-permute-start(bf16[256,256]{1,0:T(8,128)(2,1)S(1)} %copy-done.7), channel_id=1, source_target_pairs={{0,5},{1,4},{2,7},{3,6},{4,1},{5,0},{6,3},{7,2},{8,13},{9,12},{10,... | collective-permute-start | bytes 393224 | tf_op jit(solution)/shard_map/ppermute | solution.py:116
  123.1 10.9 %collective-permute-start.17 = (bf16[256,256]{1,0:T(8,128)(2,1)S(1)}, bf16[256,256]{1,0:T(8,128)(2,1)S(1)}, u32[]{:S(2)}, u32[]{:S(2)}) collective-permute-start(bf16[256,256]{1,0:T(8,128)(2,1)S(1)} %copy-done.6), channel_id=1, source_target_pairs={{0,7},{1,6},{2,5},{3,4},{4,3},{5,2},{6,1},{7,0},{8,15},{9,14},{10,... | collective-permute-start | bytes 393224 | tf_op jit(solution)/shard_map/ppermute | solution.py:116
  138.4 2.8 %collective-permute-start.18 = (f32[256,512]{1,0:T(8,128)S(1)}, f32[256,512]{1,0:T(8,128)S(1)}, u32[]{:S(2)}, u32[]{:S(2)}) collective-permute-start(f32[256,512]{1,0:T(8,128)S(1)} %get-tuple-element.64), channel_id=1, source_target_pairs={{0,8},{8,0},{16,24},{24,16},{1,9},{9,1},{17,25},{25,17},{2,10},{10... | collective-permute-start | bytes 1572872 | tf_op jit(solution)/shard_map/ppermute | solution.py:313
  140.0 10.3 %collective-permute-start.23 = (f32[768,512]{1,0:T(8,128)S(1)}, f32[768,512]{1,0:T(8,128)S(1)}, u32[]{:S(2)}, u32[]{:S(2)}) collective-permute-start(f32[768,512]{1,0:T(8,128)S(1)} %add_multiply_fusion.mine), channel_id=1, source_target_pairs={{0,8},{8,0},{16,24},{24,16},{1,9},{9,1},{17,25},{25,17},{2,10},{10... | collective-permute-start | bytes 4718600 | tf_op jit(solution)/shard_map/ppermute | solution.py:329
  141.4 7.6 %collective-permute-start.19 = (f16[256,512]{1,0:T(8,128)(2,1)S(1)}, f16[256,512]{1,0:T(8,128)(2,1)S(1)}, u32[]{:S(2)}, u32[]{:S(2)}) collective-permute-start(f16[256,512]{1,0:T(8,128)(2,1)S(1)} %add_convert_fusion.1), channel_id=1, source_target_pairs={{0,16},{8,24},{16,0},{24,8},{1,17},{9,25},{17,1},{25,9},{2,18},{10... | collective-permute-start | bytes 786440 | tf_op jit(solution)/shard_map/ppermute | solution.py:323
  149.0 4.6 %collective-permute-start.20 = (f32[256,512]{1,0:T(8,128)S(1)}, f32[256,512]{1,0:T(8,128)S(1)}, u32[]{:S(2)}, u32[]{:S(2)}) collective-permute-start(f32[256,512]{1,0:T(8,128)S(1)} %add_multiply_fusion.1.mine), channel_id=1, source_target_pairs={{0,8},{8,0},{16,24},{24,16},{1,9},{9,1},{17,25},{25,17},{2,10},{10... | collective-permute-start | bytes 1572872 | tf_op jit(solution)/shard_map/ppermute | solution.py:329

commit v5 on v4

--- a/solution.py
+++ b/solution.py
@@ -177,7 +177,7 @@
     n = len(gs)
     tokens, width = gs[0].shape
     share = anchor.shape[0]
-    block = math.gcd(size, BLOCK)
+    block = math.gcd(size, BLOCK) if size > BLOCK else TILE
     piece = min(share, block)
 
     def owned(i, info):

time: 155 us -> 156 us (level)
  no operation moved by 1% of the time
where the time goes in v5:
time: 156 us; the launch traced here: 155 us
  waiting for transfers between devices  76.2 us (49%)
  starting transfers between devices  52.1 us (33%)
  Pallas kernels  23.7 us (15%)
    ppermute x18, waiting for transfers between devices, exchange(): moved = lax.ppermute(value, 'fsdp', pairs(n, k))  64.8 us
    ppermute x18, starting transfers between devices, exchange(): moved = lax.ppermute(value, 'fsdp', pairs(n, k))  47.2 us
    pallas_call x2, Pallas kernels, inner_step(): pl.pallas_call(functools.partial(step_kernel, n, at, share, scale), grid_...  14.4 us
    ppermute x2, waiting for transfers between devices, shards(): got = lax.ppermute(half, 'worker', pairs(replicas, k))  7.27 us
    pallas_call x2, Pallas kernels, outer_step(): pl.pallas_call(functools.partial(outer_kernel, at, share), in_specs=[pl.B...  4.88 us
    pallas_call x1, Pallas kernels, split_columns(): pl.pallas_call(functools.partial(split_kernel, n, rows, pieces), in_specs...  4.47 us
    ppermute x2, waiting for transfers between devices, shards(): got = lax.ppermute(send, 'worker', pairs(replicas, 1))  4.19 us
  transfers between devices with their start and end apart: 24, of which 12 were waited for; matrix products, arithmetic and copies ran while one was open for 1% of the time, Pallas kernels for 14%

profile of v5, /device:TPU:9, one launch (start us, length us, event | category | flops | bytes accessed | tf_op | source)
XLA Modules:
  0.0 155.4 jit_solution(2447674121486674240)
XLA Ops:
  0.6 2.4 %collective-permute-start = (bf16[256,1024]{1,0:T(8,128)(2,1)}, bf16[256,1024]{1,0:T(8,128)(2,1)S(1)}, u32[]{:S(2)}, u32[]{:S(2)}) collective-permute-start(bf16[256,1024]{1,0:T(8,128)(2,1)} %bitcast.5), channel_id=1, source_target_pairs={{0,4},{1,5},{2,6},{3,7},{4,0},{5,1},{6,2},{7,3},{8,12},{9,13},{10,... | collective-permute-start | bytes 1572872 | tf_op jit(solution)/shard_map/ppermute | solution.py:116
  3.0 1.2 collective-permute-start.3
  4.2 0.2 collective-permute-start.10
  4.4 0.6 pad_add_fusion.info
  5.0 4.5 %split_columns.1 = (bf16[256,1024]{1,0:T(8,128)(2,1)}, bf16[256,1024]{1,0:T(8,128)(2,1)}, bf16[256,1024]{1,0:T(8,128)(2,1)}, bf16[256,1024]{1,0:T(8,128)(2,1)}, ...) custom-call(s32[3]{0:T(128)} %pad_add_fusion.info, ...), custom_call_target="tpu_custom_call" | custom-call | tf_op jit(solution)/shard_map/split_columns/pallas_call | solution.py:75
  9.5 0.1 collective-permute-start.11
  9.6 17.1 %collective-permute-done.refs_12_ = bf16[256,1024]{1,0:T(8,128)(2,1)S(1)} collective-permute-done((bf16[256,1024]{1,0:T(8,128)(2,1)}, bf16[256,1024]{1,0:T(8,128)(2,1)S(1)}, u32[]{:S(2)}, u32[]{:S(2)}) %collective-permute-start) | collective-permute-done | bytes 524320 | tf_op jit(solution)/shard_map/ppermute | solution.py:116
  26.7 1.1 collective-permute-start.1
  27.8 0.3 collective-permute-start.4
  28.2 0.0 collective-permute-start.6
  28.2 14.9 %collective-permute-done.11.refs_4_ = bf16[256,768]{1,0:T(8,128)(2,1)S(1)} collective-permute-done((bf16[256,768]{1,0:T(8,128)(2,1)}, bf16[256,768]{1,0:T(8,128)(2,1)S(1)}, u32[]{:S(2)}, u32[]{:S(2)}) %collective-permute-start.11) | collective-permute-done | bytes 393248 | tf_op jit(solution)/shard_map/ppermute | solution.py:116
  43.0 0.0 collective-permute-done.10.refs_10_
  43.0 1.2 collective-permute-start.12
  44.2 0.0 collective-permute-start.15
  44.2 0.0 collective-permute-done.1.refs_1_
  44.2 4.2 %collective-permute-start.2 = (bf16[256,1024]{1,0:T(8,128)(2,1)}, bf16[256,1024]{1,0:T(8,128)(2,1)S(1)}, u32[]{:S(2)}, u32[]{:S(2)}) collective-permute-start(bf16[256,1024]{1,0:T(8,128)(2,1)} %get-tuple-element.41), channel_id=1, source_target_pairs={{0,2},{1,3},{2,0},{3,1},{4,6},{5,7},{6,4},{7,5},{8,10},{9,11},{10,... | collective-permute-start | bytes 1572872 | tf_op jit(solution)/shard_map/ppermute | solution.py:116
  48.4 2.2 %collective-permute-done.4.refs_13_ = bf16[256,1024]{1,0:T(8,128)(2,1)S(1)} collective-permute-done((bf16[256,1024]{1,0:T(8,128)(2,1)S(1)}, bf16[256,1024]{1,0:T(8,128)(2,1)S(1)}, u32[]{:S(2)}, u32[]{:S(2)}) %collective-permute-start.4) | collective-permute-done | bytes 524320 | tf_op jit(solution)/shard_map/ppermute | solution.py:116
  50.6 7.9 %collective-permute-start.7 = (bf16[256,768]{1,0:T(8,128)(2,1)}, bf16[256,768]{1,0:T(8,128)(2,1)S(1)}, u32[]{:S(2)}, u32[]{:S(2)}) collective-permute-start(bf16[256,768]{1,0:T(8,128)(2,1)} %get-tuple-element.54), channel_id=1, source_target_pairs={{0,7},{1,6},{2,5},{3,4},{4,3},{5,2},{6,1},{7,0},{8,15},{9,14},{10,... | collective-permute-start | bytes 1179656 | tf_op jit(solution)/shard_map/ppermute | solution.py:116
  58.6 4.2 %collective-permute-done.15.refs_6_ = bf16[256,768]{1,0:T(8,128)(2,1)S(1)} collective-permute-done((bf16[256,768]{1,0:T(8,128)(2,1)}, bf16[256,768]{1,0:T(8,128)(2,1)S(1)}, u32[]{:S(2)}, u32[]{:S(2)}) %collective-permute-start.15) | collective-permute-done | bytes 393248 | tf_op jit(solution)/shard_map/ppermute | solution.py:116
  62.7 0.3 collective-permute-start.16
  63.0 3.4 %collective-permute-start.13 = (bf16[256,768]{1,0:T(8,128)(2,1)}, bf16[256,768]{1,0:T(8,128)(2,1)S(1)}, u32[]{:S(2)}, u32[]{:S(2)}) collective-permute-start(bf16[256,768]{1,0:T(8,128)(2,1)} %get-tuple-element.58), channel_id=1, source_target_pairs={{0,5},{1,4},{2,7},{3,6},{4,1},{5,0},{6,3},{7,2},{8,13},{9,12},{10,... | collective-permute-start | bytes 1179656 | tf_op jit(solution)/shard_map/ppermute | solution.py:116
  66.4 6.7 %collective-permute-done.7.refs_7_ = bf16[256,768]{1,0:T(8,128)(2,1)S(1)} collective-permute-done((bf16[256,768]{1,0:T(8,128)(2,1)}, bf16[256,768]{1,0:T(8,128)(2,1)S(1)}, u32[]{:S(2)}, u32[]{:S(2)}) %collective-permute-start.7) | collective-permute-done | bytes 393248 | tf_op jit(solution)/shard_map/ppermute | solution.py:116
  73.2 19.8 %collective-permute-start.8 = (bf16[256,256]{1,0:T(8,128)(2,1)}, bf16[256,256]{1,0:T(8,128)(2,1)S(1)}, u32[]{:S(2)}, u32[]{:S(2)}) collective-permute-start(bf16[256,256]{1,0:T(8,128)(2,1)} %get-tuple-element.55), channel_id=1, source_target_pairs={{0,4},{1,5},{2,6},{3,7},{4,0},{5,1},{6,2},{7,3},{8,12},{9,13},{10,... | collective-permute-start | bytes 393224 | tf_op jit(solution)/shard_map/ppermute | solution.py:116
  92.9 6.2 %collective-permute-done.13.refs_5_ = bf16[256,768]{1,0:T(8,128)(2,1)S(1)} collective-permute-done((bf16[256,768]{1,0:T(8,128)(2,1)}, bf16[256,768]{1,0:T(8,128)(2,1)S(1)}, u32[]{:S(2)}, u32[]{:S(2)}) %collective-permute-start.13) | collective-permute-done | bytes 393248 | tf_op jit(solution)/shard_map/ppermute | solution.py:116
  99.1 1.5 collective-permute-start.14
  100.6 2.6 %collective-permute-done.16.refs_15_ = bf16[256,1024]{1,0:T(8,128)(2,1)S(1)} collective-permute-done((bf16[256,1024]{1,0:T(8,128)(2,1)S(1)}, bf16[256,1024]{1,0:T(8,128)(2,1)S(1)}, u32[]{:S(2)}, u32[]{:S(2)}) %collective-permute-start.16) | collective-permute-done | bytes 524320 | tf_op jit(solution)/shard_map/ppermute | solution.py:116
  103.2 0.0 copy-start.4
  103.3 1.0 copy-done.4
  104.3 9.9 %inner_step.3 = (f32[768,512]{1,0:T(8,128)S(1)}, f32[768,512]{1,0:T(8,128)S(1)}) custom-call(s32[3]{0:T(128)S(1)} %copy-done.5, bf16[256,1024]{1,0:T(8,128)(2,1)S(1)} %copy-done.4, bf16[256,1024]{1,0:T(8,128)(2,1)S(1)} %collective-permute-done.1.refs_1_, bf16[256,1024]{1,0:T(8,128)(2,1)S(1)} %collective-permute-done.2.refs_2_, ...), custom_call_target="tpu_custom_call" | custom-call | tf_op jit(solution)/shard_map/inner_step/pallas_call | solution.py:198
  114.2 0.7 collective-permute-start.21
  114.9 3.0 %collective-permute-done.21 = f32[768,512]{1,0:T(8,128)S(1)} collective-permute-done((f32[768,512]{1,0:T(8,128)S(1)}, f32[768,512]{1,0:T(8,128)S(1)}, u32[]{:S(2)}, u32[]{:S(2)}) %collective-permute-start.21) | collective-permute-done | bytes 1572896 | tf_op jit(solution)/shard_map/ppermute | solution.py:313
  118.0 0.4 add_convert_fusion
  118.4 1.3 collective-permute-start.22
  119.6 3.5 %collective-permute-start.9 = (bf16[256,256]{1,0:T(8,128)(2,1)S(1)}, bf16[256,256]{1,0:T(8,128)(2,1)S(1)}, u32[]{:S(2)}, u32[]{:S(2)}) collective-permute-start(bf16[256,256]{1,0:T(8,128)(2,1)S(1)} %copy-done.7), channel_id=1, source_target_pairs={{0,5},{1,4},{2,7},{3,6},{4,1},{5,0},{6,3},{7,2},{8,13},{9,12},{10,... | collective-permute-start | bytes 393224 | tf_op jit(solution)/shard_map/ppermute | solution.py:116
  123.1 7.2 %collective-permute-done.9.refs_5_ = bf16[256,256]{1,0:T(8,128)(2,1)S(1)} collective-permute-done((bf16[256,256]{1,0:T(8,128)(2,1)S(1)}, bf16[256,256]{1,0:T(8,128)(2,1)S(1)}, u32[]{:S(2)}, u32[]{:S(2)}) %collective-permute-start.9) | collective-permute-done | bytes 131104 | tf_op jit(solution)/shard_map/ppermute | solution.py:116
  130.4 3.7 %collective-permute-done.17.refs_7_ = bf16[256,256]{1,0:T(8,128)(2,1)S(1)} collective-permute-done((bf16[256,256]{1,0:T(8,128)(2,1)S(1)}, bf16[256,256]{1,0:T(8,128)(2,1)S(1)}, u32[]{:S(2)}, u32[]{:S(2)}) %collective-permute-start.17) | collective-permute-done | bytes 131104 | tf_op jit(solution)/shard_map/ppermute | solution.py:116
  134.1 4.5 %inner_step.2 = (f32[256,512]{1,0:T(8,128)S(1)}, f32[256,512]{1,0:T(8,128)S(1)}) custom-call(s32[3]{0:T(128)S(1)} %copy-done.5, bf16[256,1024]{1,0:T(8,128)(2,1)S(1)} %copy-done.4, bf16[256,1024]{1,0:T(8,128)(2,1)S(1)} %collective-permute-done.1.refs_1_, bf16[256,1024]{1,0:T(8,128)(2,1)S(1)} %collective-permute-done.2.refs_2_, ...), custom_call_target="tpu_custom_call" | custom-call | tf_op jit(solution)/shard_map/inner_step/pallas_call | solution.py:198
  138.6 1.3 collective-permute-start.18
  139.8 0.3 add_multiply_fusion.mine
  140.1 0.1 collective-permute-start.23
  140.2 1.1 collective-permute-done.18
  141.4 0.1 add_convert_fusion.1
  141.5 0.3 collective-permute-start.19
  141.8 7.3 %collective-permute-done.19 = f16[256,512]{1,0:T(8,128)(2,1)S(1)} collective-permute-done((f16[256,512]{1,0:T(8,128)(2,1)S(1)}, f16[256,512]{1,0:T(8,128)(2,1)S(1)}, u32[]{:S(2)}, u32[]{:S(2)}) %collective-permute-start.19) | collective-permute-done | bytes 262176 | tf_op jit(solution)/shard_map/ppermute | solution.py:323
  149.1 0.1 add_multiply_fusion.1.mine
  149.2 1.3 collective-permute-start.20
  150.5 3.3 %outer_step.2 = (f32[1024,1024]{1,0:T(8,128)}, f32[256,1024]{1,0:T(8,128)}) custom-call(s32[3]{0:T(128)S(1)} %copy-done.5, f32[768,512]{1,0:T(8,128)S(1)} %add_multiply_fusion.mine, f32[768,512]{1,0:T(8,128)S(1)} %collective-permute-done.23.other, f32[256,1024]{1,0:T(8,128)S(1)} %copy-done, f32[256,1024]{1,0:T(8,128)S(1)} %copy-done.1), custom_call_target="tpu_custom_call" | custom-call | tf_op jit(solution)/shard_map/outer_step/pallas_call | solution.py:259
  153.8 1.5 outer_step.3
  (26 shorter events, 0.1 us)
Async XLA Ops:
  0.6 26.1 %collective-permute-start = (bf16[256,1024]{1,0:T(8,128)(2,1)}, bf16[256,1024]{1,0:T(8,128)(2,1)S(1)}, u32[]{:S(2)}, u32[]{:S(2)}) collective-permute-start(bf16[256,1024]{1,0:T(8,128)(2,1)} %bitcast.5), channel_id=1, source_target_pairs={{0,4},{1,5},{2,6},{3,7},{4,0},{5,1},{6,2},{7,3},{8,12},{9,13},{10,... | collective-permute-start | bytes 1572872 | tf_op jit(solution)/shard_map/ppermute | solution.py:116
  3.0 24.8 %collective-permute-start.3 = (bf16[256,1024]{1,0:T(8,128)(2,1)}, bf16[256,1024]{1,0:T(8,128)(2,1)S(1)}, u32[]{:S(2)}, u32[]{:S(2)}) collective-permute-start(bf16[256,1024]{1,0:T(8,128)(2,1)} %bitcast.6), channel_id=1, source_target_pairs={{0,1},{1,0},{2,3},{3,2},{4,5},{5,4},{6,7},{7,6},{8,9},{9,8},{10,11... | collective-permute-start | bytes 1572872 | tf_op jit(solution)/shard_map/ppermute | solution.py:116
  4.2 38.8 %collective-permute-start.10 = (bf16[256,1024]{1,0:T(8,128)(2,1)}, bf16[256,1024]{1,0:T(8,128)(2,1)}, u32[]{:S(2)}, u32[]{:S(2)}) collective-permute-start(bf16[256,1024]{1,0:T(8,128)(2,1)} %bitcast.7), channel_id=1, source_target_pairs={{0,2},{1,3},{2,0},{3,1},{4,6},{5,7},{6,4},{7,5},{8,10},{9,11},{10,... | collective-permute-start | bytes 1572872 | tf_op jit(solution)/shard_map/ppermute | solution.py:116
  5.0 98.2 %copy-start = (f32[256,1024]{1,0:T(8,128)S(1)}, f32[256,1024]{1,0:T(8,128)}, u32[]{:S(2)}) copy-start(f32[256,1024]{1,0:T(8,128)} %anchor.3) | copy-start | bytes 3145732
  5.0 98.2 %copy-start.1 = (f32[256,1024]{1,0:T(8,128)S(1)}, f32[256,1024]{1,0:T(8,128)}, u32[]{:S(2)}) copy-start(f32[256,1024]{1,0:T(8,128)} %momentum.3) | copy-start | bytes 3145732
  5.0 98.2 %copy-start.3 = (bf16[1,256,1024]{2,1,0:T(8,128)(2,1)S(1)}, bf16[1,256,1024]{2,1,0:T(8,128)(2,1)}, u32[]{:S(2)}) copy-start(bf16[1,256,1024]{2,1,0:T(8,128)(2,1)} %param.8) | copy-start | bytes 1572868
  5.0 98.2 %copy-start.5 = (s32[3]{0:T(128)S(1)}, s32[3]{0:T(128)}, u32[]{:S(2)}) copy-start(s32[3]{0:T(128)} %pad_add_fusion.info) | copy-start | bytes 40
  9.5 33.6 %collective-permute-start.11 = (bf16[256,768]{1,0:T(8,128)(2,1)}, bf16[256,768]{1,0:T(8,128)(2,1)S(1)}, u32[]{:S(2)}, u32[]{:S(2)}) collective-permute-start(bf16[256,768]{1,0:T(8,128)(2,1)} %get-tuple-element.47), channel_id=1, source_target_pairs={{0,4},{1,5},{2,6},{3,7},{4,0},{5,1},{6,2},{7,3},{8,12},{9,13},{10,... | collective-permute-start | bytes 1179656 | tf_op jit(solution)/shard_map/ppermute | solution.py:116
  26.7 17.6 %collective-permute-start.1 = (bf16[256,1024]{1,0:T(8,128)(2,1)}, bf16[256,1024]{1,0:T(8,128)(2,1)S(1)}, u32[]{:S(2)}, u32[]{:S(2)}) collective-permute-start(bf16[256,1024]{1,0:T(8,128)(2,1)} %get-tuple-element.39), channel_id=1, source_target_pairs={{0,1},{1,0},{2,3},{3,2},{4,5},{5,4},{6,7},{7,6},{8,9},{9,8},{10,11... | collective-permute-start | bytes 1572872 | tf_op jit(solution)/shard_map/ppermute | solution.py:116
  27.8 22.8 %collective-permute-start.4 = (bf16[256,1024]{1,0:T(8,128)(2,1)S(1)}, bf16[256,1024]{1,0:T(8,128)(2,1)S(1)}, u32[]{:S(2)}, u32[]{:S(2)}) collective-permute-start(bf16[256,1024]{1,0:T(8,128)(2,1)S(1)} %collective-permute-done.refs_12_), channel_id=1, source_target_pairs={{0,1},{1,0},{2,3},{3,2},{4,5},{5,4},{6,7},{7,6},{8,9},{9,8},{10,11... | collective-permute-start | bytes 1572872 | tf_op jit(solution)/shard_map/ppermute | solution.py:116
  28.2 22.5 %collective-permute-start.6 = (bf16[256,1024]{1,0:T(8,128)(2,1)S(1)}, bf16[256,1024]{1,0:T(8,128)(2,1)S(1)}, u32[]{:S(2)}, u32[]{:S(2)}) collective-permute-start(bf16[256,1024]{1,0:T(8,128)(2,1)S(1)} %collective-permute-done.refs_12_), channel_id=1, source_target_pairs={{0,2},{1,3},{2,0},{3,1},{4,6},{5,7},{6,4},{7,5},{8,10},{9,11},{10,... | collective-permute-start | bytes 1572872 | tf_op jit(solution)/shard_map/ppermute | solution.py:116
  43.0 20.0 %collective-permute-start.12 = (bf16[256,1024]{1,0:T(8,128)(2,1)}, bf16[256,1024]{1,0:T(8,128)(2,1)S(1)}, u32[]{:S(2)}, u32[]{:S(2)}) collective-permute-start(bf16[256,1024]{1,0:T(8,128)(2,1)} %collective-permute-done.10.refs_10_), channel_id=1, source_target_pairs={{0,1},{1,0},{2,3},{3,2},{4,5},{5,4},{6,7},{7,6},{8,9},{9,8},{10,11... | collective-permute-start | bytes 1572872 | tf_op jit(solution)/shard_map/ppermute | solution.py:116
  44.2 18.5 %collective-permute-start.15 = (bf16[256,768]{1,0:T(8,128)(2,1)}, bf16[256,768]{1,0:T(8,128)(2,1)S(1)}, u32[]{:S(2)}, u32[]{:S(2)}) collective-permute-start(bf16[256,768]{1,0:T(8,128)(2,1)} %get-tuple-element.60), channel_id=1, source_target_pairs={{0,6},{1,7},{2,4},{3,5},{4,2},{5,3},{6,0},{7,1},{8,14},{9,15},{10,... | collective-permute-start | bytes 1179656 | tf_op jit(solution)/shard_map/ppermute | solution.py:116
  44.2 56.3 %collective-permute-start.2 = (bf16[256,1024]{1,0:T(8,128)(2,1)}, bf16[256,1024]{1,0:T(8,128)(2,1)S(1)}, u32[]{:S(2)}, u32[]{:S(2)}) collective-permute-start(bf16[256,1024]{1,0:T(8,128)(2,1)} %get-tuple-element.41), channel_id=1, source_target_pairs={{0,2},{1,3},{2,0},{3,1},{4,6},{5,7},{6,4},{7,5},{8,10},{9,11},{10,... | collective-permute-start | bytes 1572872 | tf_op jit(solution)/shard_map/ppermute | solution.py:116
  50.6 50.0 %collective-permute-start.5 = (bf16[256,1024]{1,0:T(8,128)(2,1)}, bf16[256,1024]{1,0:T(8,128)(2,1)S(1)}, u32[]{:S(2)}, u32[]{:S(2)}) collective-permute-start(bf16[256,1024]{1,0:T(8,128)(2,1)} %get-tuple-element.44), channel_id=1, source_target_pairs={{0,3},{1,2},{2,1},{3,0},{4,7},{5,6},{6,5},{7,4},{8,11},{9,10},{10,... | collective-permute-start | bytes 1572872 | tf_op jit(solution)/shard_map/ppermute | solution.py:116
  50.6 22.5 %collective-permute-start.7 = (bf16[256,768]{1,0:T(8,128)(2,1)}, bf16[256,768]{1,0:T(8,128)(2,1)S(1)}, u32[]{:S(2)}, u32[]{:S(2)}) collective-permute-start(bf16[256,768]{1,0:T(8,128)(2,1)} %get-tuple-element.54), channel_id=1, source_target_pairs={{0,7},{1,6},{2,5},{3,4},{4,3},{5,2},{6,1},{7,0},{8,15},{9,14},{10,... | collective-permute-start | bytes 1179656 | tf_op jit(solution)/shard_map/ppermute | solution.py:116
  62.7 40.5 %collective-permute-start.16 = (bf16[256,1024]{1,0:T(8,128)(2,1)S(1)}, bf16[256,1024]{1,0:T(8,128)(2,1)S(1)}, u32[]{:S(2)}, u32[]{:S(2)}) collective-permute-start(bf16[256,1024]{1,0:T(8,128)(2,1)S(1)} %collective-permute-done.6.refs_14_), channel_id=1, source_target_pairs={{0,1},{1,0},{2,3},{3,2},{4,5},{5,4},{6,7},{7,6},{8,9},{9,8},{10,11... | collective-permute-start | bytes 1572872 | tf_op jit(solution)/shard_map/ppermute | solution.py:116
  63.0 36.1 %collective-permute-start.13 = (bf16[256,768]{1,0:T(8,128)(2,1)}, bf16[256,768]{1,0:T(8,128)(2,1)S(1)}, u32[]{:S(2)}, u32[]{:S(2)}) collective-permute-start(bf16[256,768]{1,0:T(8,128)(2,1)} %get-tuple-element.58), channel_id=1, source_target_pairs={{0,5},{1,4},{2,7},{3,6},{4,1},{5,0},{6,3},{7,2},{8,13},{9,12},{10,... | collective-permute-start | bytes 1179656 | tf_op jit(solution)/shard_map/ppermute | solution.py:116
  73.2 41.0 %collective-permute-start.8 = (bf16[256,256]{1,0:T(8,128)(2,1)}, bf16[256,256]{1,0:T(8,128)(2,1)S(1)}, u32[]{:S(2)}, u32[]{:S(2)}) collective-permute-start(bf16[256,256]{1,0:T(8,128)(2,1)} %get-tuple-element.55), channel_id=1, source_target_pairs={{0,4},{1,5},{2,6},{3,7},{4,0},{5,1},{6,2},{7,3},{8,12},{9,13},{10,... | collective-permute-start | bytes 393224 | tf_op jit(solution)/shard_map/ppermute | solution.py:116
  99.1 15.1 %collective-permute-start.14 = (bf16[256,256]{1,0:T(8,128)(2,1)}, bf16[256,256]{1,0:T(8,128)(2,1)S(1)}, u32[]{:S(2)}, u32[]{:S(2)}) collective-permute-start(bf16[256,256]{1,0:T(8,128)(2,1)} %get-tuple-element.59), channel_id=1, source_target_pairs={{0,6},{1,7},{2,4},{3,5},{4,2},{5,3},{6,0},{7,1},{8,14},{9,15},{10,... | collective-permute-start | bytes 393224 | tf_op jit(solution)/shard_map/ppermute | solution.py:116
  103.2 1.0 copy-start.4
  104.3 29.8 %copy-start.2 = (f32[1,1024,1024]{2,1,0:T(8,128)S(1)}, f32[1,1024,1024]{2,1,0:T(8,128)}, u32[]{:S(2)}) copy-start(f32[1,1024,1024]{2,1,0:T(8,128)} %refs_16_.3) | copy-start | bytes 12582916
  114.2 5.4 %copy-start.7 = (bf16[256,256]{1,0:T(8,128)(2,1)S(1)}, bf16[256,256]{1,0:T(8,128)(2,1)}, u32[]{:S(2)}) copy-start(bf16[256,256]{1,0:T(8,128)(2,1)} %get-tuple-element.56) | copy-start | bytes 393220
  114.2 8.9 %copy-start.6 = (bf16[256,256]{1,0:T(8,128)(2,1)S(1)}, bf16[256,256]{1,0:T(8,128)(2,1)}, u32[]{:S(2)}) copy-start(bf16[256,256]{1,0:T(8,128)(2,1)} %get-tuple-element.62) | copy-start | bytes 393220
  114.2 3.8 %collective-permute-start.21 = (f32[768,512]{1,0:T(8,128)S(1)}, f32[768,512]{1,0:T(8,128)S(1)}, u32[]{:S(2)}, u32[]{:S(2)}) collective-permute-start(f32[768,512]{1,0:T(8,128)S(1)} %get-tuple-element.68), channel_id=1, source_target_pairs={{0,8},{8,0},{16,24},{24,16},{1,9},{9,1},{17,25},{25,17},{2,10},{10... | collective-permute-start | bytes 4718600 | tf_op jit(solution)/shard_map/ppermute | solution.py:313
  118.4 21.5 %collective-permute-start.22 = (f16[768,512]{1,0:T(8,128)(2,1)S(1)}, f16[768,512]{1,0:T(8,128)(2,1)S(1)}, u32[]{:S(2)}, u32[]{:S(2)}) collective-permute-start(f16[768,512]{1,0:T(8,128)(2,1)S(1)} %add_convert_fusion), channel_id=1, source_target_pairs={{0,16},{8,24},{16,0},{24,8},{1,17},{9,25},{17,1},{25,9},{2,18},{10... | collective-permute-start | bytes 2359304 | tf_op jit(solution)/shard_map/ppermute | solution.py:323
  119.6 10.7 %collective-permute-start.9 = (bf16[256,256]{1,0:T(8,128)(2,1)S(1)}, bf16[256,256]{1,0:T(8,128)(2,1)S(1)}, u32[]{:S(2)}, u32[]{:S(2)}) collective-permute-start(bf16[256,256]{1,0:T(8,128)(2,1)S(1)} %copy-done.7), channel_id=1, source_target_pairs={{0,5},{1,4},{2,7},{3,6},{4,1},{5,0},{6,3},{7,2},{8,13},{9,12},{10,... | collective-permute-start | bytes 393224 | tf_op jit(solution)/shard_map/ppermute | solution.py:116
  123.1 10.9 %collective-permute-start.17 = (bf16[256,256]{1,0:T(8,128)(2,1)S(1)}, bf16[256,256]{1,0:T(8,128)(2,1)S(1)}, u32[]{:S(2)}, u32[]{:S(2)}) collective-permute-start(bf16[256,256]{1,0:T(8,128)(2,1)S(1)} %copy-done.6), channel_id=1, source_target_pairs={{0,7},{1,6},{2,5},{3,4},{4,3},{5,2},{6,1},{7,0},{8,15},{9,14},{10,... | collective-permute-start | bytes 393224 | tf_op jit(solution)/shard_map/ppermute | solution.py:116
  138.6 2.8 %collective-permute-start.18 = (f32[256,512]{1,0:T(8,128)S(1)}, f32[256,512]{1,0:T(8,128)S(1)}, u32[]{:S(2)}, u32[]{:S(2)}) collective-permute-start(f32[256,512]{1,0:T(8,128)S(1)} %get-tuple-element.64), channel_id=1, source_target_pairs={{0,8},{8,0},{16,24},{24,16},{1,9},{9,1},{17,25},{25,17},{2,10},{10... | collective-permute-start | bytes 1572872 | tf_op jit(solution)/shard_map/ppermute | solution.py:313
  140.1 10.3 %collective-permute-start.23 = (f32[768,512]{1,0:T(8,128)S(1)}, f32[768,512]{1,0:T(8,128)S(1)}, u32[]{:S(2)}, u32[]{:S(2)}) collective-permute-start(f32[768,512]{1,0:T(8,128)S(1)} %add_multiply_fusion.mine), channel_id=1, source_target_pairs={{0,8},{8,0},{16,24},{24,16},{1,9},{9,1},{17,25},{25,17},{2,10},{10... | collective-permute-start | bytes 4718600 | tf_op jit(solution)/shard_map/ppermute | solution.py:329
  141.5 7.6 %collective-permute-start.19 = (f16[256,512]{1,0:T(8,128)(2,1)S(1)}, f16[256,512]{1,0:T(8,128)(2,1)S(1)}, u32[]{:S(2)}, u32[]{:S(2)}) collective-permute-start(f16[256,512]{1,0:T(8,128)(2,1)S(1)} %add_convert_fusion.1), channel_id=1, source_target_pairs={{0,16},{8,24},{16,0},{24,8},{1,17},{9,25},{17,1},{25,9},{2,18},{10... | collective-permute-start | bytes 786440 | tf_op jit(solution)/shard_map/ppermute | solution.py:323
  149.2 4.6 %collective-permute-start.20 = (f32[256,512]{1,0:T(8,128)S(1)}, f32[256,512]{1,0:T(8,128)S(1)}, u32[]{:S(2)}, u32[]{:S(2)}) collective-permute-start(f32[256,512]{1,0:T(8,128)S(1)} %add_multiply_fusion.1.mine), channel_id=1, source_target_pairs={{0,8},{8,0},{16,24},{24,16},{1,9},{9,1},{17,25},{25,17},{2,10},{10... | collective-permute-start | bytes 1572872 | tf_op jit(solution)/shard_map/ppermute | solution.py:329
